TPU v7x, 512 devices: a whole 4x8x8 slice. The times are simulated.
512 devices in a mesh: ctx: 128 (over z_hi, y, x), ch: 4 (over z_lo, core).
Axes of the slice: x: 4, y: 8, z: 8 (z_hi: 4, z_lo: 2; z = z_hi * 2 + z_lo), core: 2. Of those that a mesh axis runs over, the one named last changes fastest.
Arguments:
- gate_in: bfloat16 [16384, 4096], P('ctx', 'ch'), may hold values from -6 to 6
- values: bfloat16 [16384, 4096], P('ctx', 'ch'), may hold values from -6 to 6
- filters: float32 [16384, 1024], P('ctx'), may hold values from -0.046875 to 0.046875
- out_grad: bfloat16 [16384, 4096], P('ctx', 'ch'), may hold values from -6 to 6
Outputs:
- gate_grad: float32 [16384, 4096], P('ctx', 'ch')
- value_grad: float32 [16384, 4096], P('ctx', 'ch')
- filter_grad: float32 [16384, 1024], P('ctx', 'ch')
All inputs are finite; a program needn't handle non-finite values.
Results may differ from a plain program's by a relative error of at most 0.0029.
Values sent between devices are 32-bit elements; how exact they have to be, the bound alone decides.
A program may use at most 64 MiB of HBM per device.

v0:
```python
import math

import jax
import jax.numpy as jnp
from jax import lax
from jax.sharding import PartitionSpec as P

TWO_PI = 2.0 * math.pi


def per_device(gate_in, values, filters, out_grad):
    highest = lax.Precision.HIGHEST
    rows, width = values.shape
    ctx_count = lax.axis_size("ctx")
    ctx_index = lax.axis_index("ctx")
    ch_count = lax.axis_size("ch")
    stride = rows // ctx_count
    outer_len = 2 * ctx_count
    padded = outer_len * rows
    slot_index = jnp.arange(outer_len, dtype=jnp.int32)
    slot_owner = slot_index // 2
    slot_parity = slot_index % 2
    block_freq = jnp.where(
        slot_owner == 0,
        slot_parity * ctx_count,
        jnp.where(slot_parity == 0, slot_owner, outer_len - slot_owner),
    )
    block_pos = jnp.arange(ctx_count, dtype=jnp.int32)
    outer_angle = (
        TWO_PI
        * (block_freq[:, None] * block_pos[None, :] % outer_len).astype(jnp.float32)
        / outer_len
    )
    outer_cos = jnp.cos(outer_angle)
    outer_sin = jnp.sin(outer_angle)
    row_pos = ctx_index * stride + jnp.arange(stride, dtype=jnp.int32)
    twist_angle = (
        TWO_PI * (block_freq[:, None] * row_pos[None, :] % padded).astype(jnp.float32) / padded
    )
    twist_cos = jnp.cos(twist_angle)[:, :, None]
    twist_sin = jnp.sin(twist_angle)[:, :, None]
    inner_pos = jnp.arange(rows, dtype=jnp.int32)
    inner_angle = (
        TWO_PI * (inner_pos[:, None] * inner_pos[None, :] % rows).astype(jnp.float32) / rows
    )
    inner_cos = jnp.cos(inner_angle)
    inner_sin = jnp.sin(inner_angle)
    outer_fwd = jnp.stack([jnp.stack([outer_cos, outer_sin]), jnp.stack([-outer_sin, outer_cos])])
    outer_inv = jnp.stack(
        [jnp.stack([outer_cos.T, -outer_sin.T]), jnp.stack([outer_sin.T, outer_cos.T])]
    )
    inner_fwd = jnp.stack([jnp.stack([inner_cos, inner_sin]), jnp.stack([-inner_sin, inner_cos])])
    inner_inv = jnp.stack([jnp.stack([inner_cos, -inner_sin]), jnp.stack([inner_sin, inner_cos])])

    def forward(stacked):
        members, _, cols = stacked.shape
        moved = lax.all_to_all(
            stacked.reshape(members, 1, rows, cols), "ctx", split_axis=2, concat_axis=1, tiled=True
        )
        flat_rows = moved.reshape(members, ctx_count, stride * cols)
        first = jnp.einsum("rmkn,mnq->rkq", outer_fwd[:, :members], flat_rows, precision=highest)
        first = first.reshape(2, outer_len, stride, cols)
        turned = jnp.stack(
            [
                first[0] * twist_cos + first[1] * twist_sin,
                first[1] * twist_cos - first[0] * twist_sin,
            ]
        )
        arrived = lax.all_to_all(turned, "ctx", split_axis=1, concat_axis=2, tiled=True)
        spec = jnp.einsum("abkn,bfnc->afkc", inner_fwd, arrived, precision=highest)
        return (spec[0], spec[1])

    def inverse(spec_re, spec_im, members):
        back = jnp.einsum(
            "abkn,bfnc->afkc", inner_inv, jnp.stack([spec_re, spec_im]), precision=highest
        )
        cols = back.shape[3]
        arrived = lax.all_to_all(back, "ctx", split_axis=2, concat_axis=1, tiled=True)
        recv_re = arrived[0]
        recv_im = arrived[1]
        untwisted = jnp.stack(
            [recv_re * twist_cos - recv_im * twist_sin, recv_re * twist_sin + recv_im * twist_cos]
        ).reshape(2, outer_len, stride * cols)
        result = (
            jnp.einsum("mrnk,rkq->mnq", outer_inv[:members], untwisted, precision=highest) / padded
        )
        result = result.reshape(members, ctx_count, stride, cols)
        landed = lax.all_to_all(result, "ctx", split_axis=1, concat_axis=2, tiled=True)
        return landed.reshape(members, rows, cols)

    def mirror(spectrum):
        general = spectrum[::-1, ::-1]
        first = jnp.stack([jnp.roll(spectrum[0, ::-1], 1, axis=0), spectrum[1, ::-1]])
        return jnp.where(ctx_index == 0, first, general)

    grad_wide = out_grad.astype(jnp.float32)
    inner_low = (grad_wide * gate_in.astype(jnp.float32)).astype(jnp.bfloat16)
    inner_low = lax.optimization_barrier(inner_low)
    joint_re, joint_im = forward(
        jnp.stack([values.astype(jnp.float32), inner_low.astype(jnp.float32)])
    )
    mirror_re = mirror(joint_re)
    mirror_im = mirror(joint_im)
    value_re = (joint_re + mirror_re) * 0.5
    value_im = (joint_im - mirror_im) * 0.5
    inner_re = (joint_im + mirror_im) * 0.5
    inner_im = (mirror_re - joint_re) * 0.5
    filt_re, filt_im = forward(filters[None])
    conv_re = filt_re * value_re - filt_im * value_im
    conv_im = filt_re * value_im + filt_im * value_re
    back_re = filt_re * inner_re + filt_im * inner_im
    back_im = filt_re * inner_im - filt_im * inner_re
    both = inverse(conv_re - back_im, conv_im + back_re, 2)
    conv_out = both[0]
    value_grad = both[1]
    gate_grad = grad_wide * conv_out
    terms_re = value_re * inner_re + value_im * inner_im
    terms_im = value_re * inner_im - value_im * inner_re
    factor = 1.0 / math.sqrt(ch_count * rows * ctx_count)
    local_terms = inverse(terms_re, terms_im, 1)[0]
    filter_grad = lax.psum_scatter(local_terms, "ch", scatter_dimension=1, tiled=True) * factor
    return (gate_grad, value_grad, filter_grad)


def solution(mesh):
    return jax.shard_map(
        per_device,
        mesh=mesh,
        in_specs=(P("ctx", "ch"), P("ctx", "ch"), P("ctx", None), P("ctx", "ch")),
        out_specs=(P("ctx", "ch"), P("ctx", "ch"), P("ctx", "ch")),
        check_vma=False,
    )
```

profile of v0, /device:TPU:1, one launch (start us, length us, event | category | flops | bytes accessed | tf_op | source)
XLA Modules:
  0.0 459.4 jit_solution(129600212974417945)
XLA Ops:
  9.5 20.8 %all-to-all-start = ((f32[1,1,128,1024]{3,1,0,2:T(1,128)}), f32[1,1,128,1024]{3,1,0,2:T(1,128)S(1)}, u32[]{:S(2)}, u32[]{:S(2)}) async-start(f32[1,1,128,1024]{3,1,0,2:T(1,128)} %reshape_broadcast_in_dim.3), calls=%async_computation | async-start | bytes 1048576 | tf_op jit(solution)/shard_map/all_to_all | solution.py:57
  32.3 16.7 %all-to-all-done = f32[1,1,128,1024]{3,1,0,2:T(1,128)S(1)} async-done(((f32[1,1,128,1024]{3,1,0,2:T(1,128)}), f32[1,1,128,1024]{3,1,0,2:T(1,128)S(1)}, u32[]{:S(2)}, u32[]{:S(2)}) %all-to-all-start) | async-done | bytes 524320 | tf_op jit(solution)/shard_map/all_to_all | solution.py:57
  49.0 9.0 %all-to-all-start.2 = ((f32[2,1,128,1024]{3,0,1,2:T(2,128)}), f32[2,1,128,1024]{3,0,1,2:T(2,128)S(1)}, u32[]{:S(2)}, u32[]{:S(2)}) async-start(f32[2,1,128,1024]{3,0,1,2:T(2,128)} %copy.37), calls=%async_computation.2 | async-start | bytes 2097152 | tf_op jit(solution)/shard_map/all_to_all | solution.py:57
  62.3 24.6 %all-to-all-done.2 = f32[2,1,128,1024]{3,0,1,2:T(2,128)S(1)} async-done(((f32[2,1,128,1024]{3,0,1,2:T(2,128)}), f32[2,1,128,1024]{3,0,1,2:T(2,128)S(1)}, u32[]{:S(2)}, u32[]{:S(2)}) %all-to-all-start.2) | async-done | bytes 1048608 | tf_op jit(solution)/shard_map/all_to_all | solution.py:57
  91.9 3.5 copy.39
  95.4 9.9 %all-to-all-start.3 = ((f32[2,256,1,1024]{3,2,0,1:T(1,128)}), f32[2,256,1,1024]{3,2,0,1:T(1,128)S(1)}, u32[]{:S(2)}, u32[]{:S(2)}) async-start(f32[2,256,1,1024]{3,2,0,1:T(1,128)} %copy.39), calls=%async_computation.3 | async-start | bytes 4194304 | tf_op jit(solution)/shard_map/all_to_all | solution.py:69
  106.7 3.5 copy.34
  110.2 47.3 %all-to-all-done.3 = f32[2,256,1,1024]{3,2,0,1:T(1,128)S(1)} async-done(((f32[2,256,1,1024]{3,2,0,1:T(1,128)}), f32[2,256,1,1024]{3,2,0,1:T(1,128)S(1)}, u32[]{:S(2)}, u32[]{:S(2)}) %all-to-all-start.3) | async-done | bytes 2097184 | tf_op jit(solution)/shard_map/all_to_all | solution.py:69
  157.5 10.4 %all-to-all-start.1 = ((f32[2,256,1,1024]{3,2,0,1:T(1,128)}), f32[2,256,1,1024]{3,2,0,1:T(1,128)}, u32[]{:S(2)}, u32[]{:S(2)}) async-start(f32[2,256,1,1024]{3,2,0,1:T(1,128)} %copy.34), calls=%async_computation.1 | async-start | bytes 4194304 | tf_op jit(solution)/shard_map/all_to_all | solution.py:69
  169.6 4.2 fusion.24
  174.9 5.7 %rev.17 = f32[2,128,1024]{1,2,0:T(8,128)} reverse(f32[2,128,1024]{1,2,0:T(8,128)S(1)} %get-tuple-element.28), dimensions={0,1} | reverse | bytes 2097152 | tf_op jit(solution)/shard_map/rev | solution.py:92
  181.8 5.0 %rev.16 = f32[1,128,1024]{1,2,0:T(8,128)} reverse(f32[1,128,1024]{1,2,0:T(8,128)} %get-tuple-element.24), dimensions={1} | reverse | bytes 1048576 | tf_op jit(solution)/shard_map/rev | solution.py:93
  187.8 5.0 %slice.145 = f32[1,127,1024]{1,2,0:T(8,128)} reverse(f32[1,127,1024]{1,2,0:T(8,128)} %slice.169), dimensions={1} | reverse | bytes 1040384 | tf_op jit(solution)/shard_map/jit(_roll_static)/slice | solution.py:93
  192.8 9.3 %rev.15 = f32[2,128,1024]{1,2,0:T(8,128)} reverse(f32[2,128,1024]{1,2,0:T(8,128)} %get-tuple-element.27), dimensions={0,1} | reverse | bytes 2097152 | tf_op jit(solution)/shard_map/rev | solution.py:92
  202.0 5.0 %rev.14 = f32[1,128,1024]{1,2,0:T(8,128)} reverse(f32[1,128,1024]{1,2,0:T(8,128)} %get-tuple-element.26), dimensions={1} | reverse | bytes 1048576 | tf_op jit(solution)/shard_map/rev | solution.py:93
  208.0 5.0 %slice.134 = f32[1,127,1024]{1,2,0:T(8,128)} reverse(f32[1,127,1024]{1,2,0:T(8,128)} %slice.163), dimensions={1} | reverse | bytes 1040384 | tf_op jit(solution)/shard_map/jit(_roll_static)/slice | solution.py:93
  213.9 5.7 %all-to-all-done.1 = f32[2,256,1,1024]{3,2,0,1:T(1,128)} async-done(((f32[2,256,1,1024]{3,2,0,1:T(1,128)}), f32[2,256,1,1024]{3,2,0,1:T(1,128)}, u32[]{:S(2)}, u32[]{:S(2)}) %all-to-all-start.1) | async-done | bytes 2097184 | tf_op jit(solution)/shard_map/all_to_all | solution.py:69
  219.6 4.0 copy.65
  223.6 4.3 copy.35
  227.9 3.6 fusion.21
  239.7 9.9 %all-to-all-start.6 = ((f32[2,2,128,1024]{3,0,1,2:T(2,128)}), f32[2,2,128,1024]{3,0,1,2:T(2,128)S(1)}, u32[]{:S(2)}, u32[]{:S(2)}) async-start(f32[2,2,128,1024]{3,0,1,2:T(2,128)} %copy.47), calls=%async_computation.6 | async-start | bytes 4194304 | tf_op jit(solution)/shard_map/all_to_all | solution.py:78
  249.6 4.4 fusion.15
  254.1 4.2 copy.43
  258.3 43.1 %all-to-all-done.6 = f32[2,2,128,1024]{3,0,1,2:T(2,128)S(1)} async-done(((f32[2,2,128,1024]{3,0,1,2:T(2,128)}), f32[2,2,128,1024]{3,0,1,2:T(2,128)S(1)}, u32[]{:S(2)}, u32[]{:S(2)}) %all-to-all-start.6) | async-done | bytes 2097184 | tf_op jit(solution)/shard_map/all_to_all | solution.py:78
  301.4 9.5 %all-to-all-start.4 = ((f32[2,2,128,1024]{3,0,1,2:T(2,128)}), f32[2,2,128,1024]{3,0,1,2:T(2,128)}, u32[]{:S(2)}, u32[]{:S(2)}) async-start(f32[2,2,128,1024]{3,0,1,2:T(2,128)} %copy.43), calls=%async_computation.4 | async-start | bytes 4194304 | tf_op jit(solution)/shard_map/all_to_all | solution.py:78
  311.4 7.8 %slice_reduce_fusion.1 = (f32[128,2,1024]{2,1,0:T(2,128)}, f32[128,2,1024]{2,1,0:T(2,128)}) fusion(f32[2,128,2,1,1024]{4,0,2,1,3:T(2,128)S(1)} %bitcast.231), kind=kLoop, calls=%fused_computation.33 | loop fusion | bytes 4194304 | tf_op jit(solution)/shard_map/slice | solution.py:79
  322.9 39.5 %all-to-all-done.4 = f32[2,2,128,1024]{3,0,1,2:T(2,128)} async-done(((f32[2,2,128,1024]{3,0,1,2:T(2,128)}), f32[2,2,128,1024]{3,0,1,2:T(2,128)}, u32[]{:S(2)}, u32[]{:S(2)}) %all-to-all-start.4) | async-done | bytes 2097184 | tf_op jit(solution)/shard_map/all_to_all | solution.py:78
  362.4 9.4 %slice_reduce_fusion.3 = (f32[128,2,1024]{2,1,0:T(2,128)S(1)}, f32[128,2,1024]{2,1,0:T(2,128)S(1)}) fusion(f32[2,128,2,1,1024]{4,0,2,1,3:T(2,128)} %bitcast.59), kind=kLoop, calls=%fused_computation.35 | loop fusion | bytes 4194304 | tf_op jit(solution)/shard_map/slice | solution.py:79
  380.3 9.5 %all-to-all-start.7 = ((f32[1,128,1,1024]{3,2,0,1:T(1,128)}), f32[1,128,1,1024]{3,2,0,1:T(1,128)S(1)}, u32[]{:S(2)}, u32[]{:S(2)}) async-start(f32[1,128,1,1024]{3,2,0,1:T(1,128)} %copy.48), calls=%async_computation.7 | async-start | bytes 1048576 | tf_op jit(solution)/shard_map/all_to_all | solution.py:88
  393.9 13.4 %all-to-all-done.7 = f32[1,128,1,1024]{3,2,0,1:T(1,128)S(1)} async-done(((f32[1,128,1,1024]{3,2,0,1:T(1,128)}), f32[1,128,1,1024]{3,2,0,1:T(1,128)S(1)}, u32[]{:S(2)}, u32[]{:S(2)}) %all-to-all-start.7) | async-done | bytes 524320 | tf_op jit(solution)/shard_map/all_to_all | solution.py:88
  407.3 9.5 %all-to-all-start.5 = ((f32[2,128,1,1024]{3,2,0,1:T(1,128)}), f32[2,128,1,1024]{3,2,0,1:T(1,128)S(1)}, u32[]{:S(2)}, u32[]{:S(2)}) async-start(f32[2,128,1,1024]{3,2,0,1:T(1,128)} %copy.44), calls=%async_computation.5 | async-start | bytes 2097152 | tf_op jit(solution)/shard_map/all_to_all | solution.py:88
  417.7 27.4 %all-to-all-done.5 = f32[2,128,1,1024]{3,2,0,1:T(1,128)S(1)} async-done(((f32[2,128,1,1024]{3,2,0,1:T(1,128)}), f32[2,128,1,1024]{3,2,0,1:T(1,128)S(1)}, u32[]{:S(2)}, u32[]{:S(2)}) %all-to-all-start.5) | async-done | bytes 1048608 | tf_op jit(solution)/shard_map/all_to_all | solution.py:88
  (78 shorter events, 54.5 us)
Async XLA Ops:
  7.2 23.1 %copy-start.11 = (bf16[128,1024]{1,0:T(8,128)(2,1)S(1)}, bf16[128,1024]{1,0:T(8,128)(2,1)}, u32[]{:S(2)}) copy-start(bf16[128,1024]{1,0:T(8,128)(2,1)} %param.7) | copy-start | bytes 786436
  7.2 23.1 %copy-start.13 = (bf16[128,1024]{1,0:T(8,128)(2,1)S(1)}, bf16[128,1024]{1,0:T(8,128)(2,1)}, u32[]{:S(2)}) copy-start(bf16[128,1024]{1,0:T(8,128)(2,1)} %param.4) | copy-start | bytes 786436
  7.2 23.2 %copy-start.14 = (bf16[128,1024]{1,0:T(8,128)(2,1)S(1)}, bf16[128,1024]{1,0:T(8,128)(2,1)}, u32[]{:S(2)}) copy-start(bf16[128,1024]{1,0:T(8,128)(2,1)} %param.5) | copy-start | bytes 786436
  9.5 39.5 %all-to-all-start = ((f32[1,1,128,1024]{3,1,0,2:T(1,128)}), f32[1,1,128,1024]{3,1,0,2:T(1,128)S(1)}, u32[]{:S(2)}, u32[]{:S(2)}) async-start(f32[1,1,128,1024]{3,1,0,2:T(1,128)} %reshape_broadcast_in_dim.3), calls=%async_computation | async-start | bytes 1048576 | tf_op jit(solution)/shard_map/all_to_all | solution.py:57
  49.0 9.7 %copy-start.9 = (f32[1,1,128,1024]{3,1,0,2:T(1,128)}, f32[1,1,128,1024]{3,1,0,2:T(1,128)S(1)}, u32[]{:S(2)}) copy-start(f32[1,1,128,1024]{3,1,0,2:T(1,128)S(1)} %all-to-all-done) | copy-start | bytes 1572868
  49.0 37.9 %all-to-all-start.2 = ((f32[2,1,128,1024]{3,0,1,2:T(2,128)}), f32[2,1,128,1024]{3,0,1,2:T(2,128)S(1)}, u32[]{:S(2)}, u32[]{:S(2)}) async-start(f32[2,1,128,1024]{3,0,1,2:T(2,128)} %copy.37), calls=%async_computation.2 | async-start | bytes 2097152 | tf_op jit(solution)/shard_map/all_to_all | solution.py:57
  58.7 0.7 copy-start.3
  95.4 62.0 %all-to-all-start.3 = ((f32[2,256,1,1024]{3,2,0,1:T(1,128)}), f32[2,256,1,1024]{3,2,0,1:T(1,128)S(1)}, u32[]{:S(2)}, u32[]{:S(2)}) async-start(f32[2,256,1,1024]{3,2,0,1:T(1,128)} %copy.39), calls=%async_computation.3 | async-start | bytes 4194304 | tf_op jit(solution)/shard_map/all_to_all | solution.py:69
  157.5 62.2 %all-to-all-start.1 = ((f32[2,256,1,1024]{3,2,0,1:T(1,128)}), f32[2,256,1,1024]{3,2,0,1:T(1,128)}, u32[]{:S(2)}, u32[]{:S(2)}) async-start(f32[2,256,1,1024]{3,2,0,1:T(1,128)} %copy.34), calls=%async_computation.1 | async-start | bytes 4194304 | tf_op jit(solution)/shard_map/all_to_all | solution.py:69
  168.5 1.1 copy-start.10
  227.9 3.7 copy-start.6
  227.9 3.7 copy-start.8
  227.9 3.9 copy-start.7
  231.6 1.2 copy-start
  231.6 1.5 copy-start.1
  231.6 1.7 copy-start.4
  231.6 1.8 copy-start.5
  239.7 61.6 %all-to-all-start.6 = ((f32[2,2,128,1024]{3,0,1,2:T(2,128)}), f32[2,2,128,1024]{3,0,1,2:T(2,128)S(1)}, u32[]{:S(2)}, u32[]{:S(2)}) async-start(f32[2,2,128,1024]{3,0,1,2:T(2,128)} %copy.47), calls=%async_computation.6 | async-start | bytes 4194304 | tf_op jit(solution)/shard_map/all_to_all | solution.py:78
  301.4 61.0 %all-to-all-start.4 = ((f32[2,2,128,1024]{3,0,1,2:T(2,128)}), f32[2,2,128,1024]{3,0,1,2:T(2,128)}, u32[]{:S(2)}, u32[]{:S(2)}) async-start(f32[2,2,128,1024]{3,0,1,2:T(2,128)} %copy.43), calls=%async_computation.4 | async-start | bytes 4194304 | tf_op jit(solution)/shard_map/all_to_all | solution.py:78
  319.1 2.0 copy-start.2
  380.3 26.9 %all-to-all-start.7 = ((f32[1,128,1,1024]{3,2,0,1:T(1,128)}), f32[1,128,1,1024]{3,2,0,1:T(1,128)S(1)}, u32[]{:S(2)}, u32[]{:S(2)}) async-start(f32[1,128,1,1024]{3,2,0,1:T(1,128)} %copy.48), calls=%async_computation.7 | async-start | bytes 1048576 | tf_op jit(solution)/shard_map/all_to_all | solution.py:88
  407.3 37.9 %all-to-all-start.5 = ((f32[2,128,1,1024]{3,2,0,1:T(1,128)}), f32[2,128,1,1024]{3,2,0,1:T(1,128)S(1)}, u32[]{:S(2)}, u32[]{:S(2)}) async-start(f32[2,128,1,1024]{3,2,0,1:T(1,128)} %copy.44), calls=%async_computation.5 | async-start | bytes 2097152 | tf_op jit(solution)/shard_map/all_to_all | solution.py:88
  416.7 33.8 %reduce-scatter.2.cloned.1.call-start = ((), (), s32[]{:S(2)}) async-start(), calls=%async_computation.9 | async-start | bytes 655360 | tf_op jit(solution)/shard_map/reduce_scatter | solution.py:121
  417.7 29.1 %copy-start.12 = (bf16[128,1024]{1,0:T(8,128)(2,1)S(1)}, bf16[128,1024]{1,0:T(8,128)(2,1)}, u32[]{:S(2)}) copy-start(bf16[128,1024]{1,0:T(8,128)(2,1)} %param.7) | copy-start | bytes 786436
Sparse Core Ops, SparseCore 0:
  420.4 30.0 reduce-scatter.1
where the time goes:
time: 468 us; the launch traced here: 459 us
  waiting for transfers between devices  221 us (47%)
  local copies, waits for them, and re-layouts  99.4 us (21%)
  starting transfers between devices  88.5 us (19%)
  matrix products  23.2 us (5%)
  between operations  14.9 us (3%)
  other arithmetic  12.9 us (3%)
    all_to_all x2, waiting for transfers between devices, inverse(): lax.all_to_all(back, 'ctx', split_axis=2, concat_axis=1, tiled=True)  82.6 us
    all_to_all x2, waiting for transfers between devices, forward(): lax.all_to_all(turned, 'ctx', split_axis=1, concat_axis=2, tiled=True)  52.9 us
    all_to_all x2, waiting for transfers between devices, forward(): lax.all_to_all(stacked.reshape(members, 1, rows, cols), 'ctx', split_axis...  41.3 us
    all_to_all x2, waiting for transfers between devices, inverse(): lax.all_to_all(result, 'ctx', split_axis=1, concat_axis=2, tiled=True)  40.8 us
    all_to_all x2, starting transfers between devices, forward(): lax.all_to_all(stacked.reshape(members, 1, rows, cols), 'ctx', split_axis...  29.8 us
    all_to_all x2, starting transfers between devices, forward(): lax.all_to_all(turned, 'ctx', split_axis=1, concat_axis=2, tiled=True)  20.3 us
    all_to_all x2, starting transfers between devices, inverse(): lax.all_to_all(back, 'ctx', split_axis=2, concat_axis=1, tiled=True)  19.4 us
    all_to_all x2, starting transfers between devices, inverse(): lax.all_to_all(result, 'ctx', split_axis=1, concat_axis=2, tiled=True)  19 us
  transfers between devices with their start and end apart: 9, of which 9 were waited for; matrix products, arithmetic and copies ran while one was open for 18% of the time, Pallas kernels for 0%

commit v1 on v0

v1 whole, which is shorter than its diff:
```python
import functools

import jax
import jax.numpy as jnp
from jax import lax
from jax.experimental import pallas as pl
from jax.experimental.pallas import tpu as pltpu
from jax.sharding import PartitionSpec as P

BF = jnp.bfloat16
F32 = jnp.float32
MESH = pl.DeviceIdType.MESH
VM = pl.BlockSpec(memory_space=pltpu.VMEM)


def dot(a, b, ca=1, cb=0):
    return lax.dot_general(a, b, (((ca,), (cb,)), ((), ())), preferred_element_type=F32)


def coords():
    ctx = lax.axis_index("ctx")
    ch = lax.axis_index("ch")
    return ctx % 4, (ctx // 4) % 8, (ctx // 32) * 2 + ch // 2, ch % 2


def peer(x, y, z, c):
    return (z // 2) * 32 + y * 4 + x, (z % 2) * 2 + c


def place(ctx, ch):
    return (ctx % 2) * 256 + (ctx // 2) * 4 + ch


def pack_kernel(gate_ref, values_ref, filters_ref, grad_ref, x_ref, f_ref, wide):
    inner = (grad_ref[...].astype(F32) * gate_ref[...].astype(F32)).astype(BF)
    for s, signal in enumerate((values_ref[...], inner)):
        wide[...] = signal.astype(F32).T
        for p in range(2):
            x_ref[pl.ds(2 * s + p, 512, stride=4), :] = wide[pl.ds(p, 512, stride=2), :]
    start = pl.multiple_of(lax.axis_index("ch") * 256, 256)
    f_ref[...] = filters_ref[:, pl.ds(start, 256)].T


def gather_kernel(x_ref, f_ref, ox_ref, of_ref, lx, lf, sx, rx, sf, rf):
    x, y, z, c = coords()
    ctx, ch = peer(x, y, z, c)
    row = place(ctx, ch)
    own_x = pltpu.make_async_copy(x_ref.at[ch * 128 + ctx], ox_ref.at[row], lx)
    own_f = pltpu.make_async_copy(f_ref.at[ctx], of_ref.at[ctx], lf)
    own_x.start()
    own_f.start()

    def body(i, _):
        x2 = (x + i // 128) % 4
        y2 = (y + i // 2) % 8
        z2 = (z + i // 16) % 8
        c2 = (c + i) % 2
        ctx2, ch2 = peer(x2, y2, z2, c2)
        pltpu.make_async_remote_copy(
            x_ref.at[ch2 * 128 + ctx2], ox_ref.at[row], sx, rx, device_id=(ctx2, ch2), device_id_type=MESH
        ).start()
        return 0

    lax.fori_loop(1, 512, body, 0)

    def body_f(i, _):
        ctx2 = (ctx + i) % 128
        pltpu.make_async_remote_copy(
            f_ref.at[ctx2], of_ref.at[ctx], sf, rf, device_id=(ctx2, ch), device_id_type=MESH
        ).start()
        return 0

    lax.fori_loop(1, 128, body_f, 0)
    own_x.wait()
    own_f.wait()
    for sem in (sx, rx):
        pltpu.make_async_copy(x_ref.at[pl.ds(0, 511)], ox_ref.at[pl.ds(0, 511)], sem).wait()
    for sem in (sf, rf):
        pltpu.make_async_copy(f_ref.at[pl.ds(0, 127)], of_ref.at[pl.ds(0, 127)], sem).wait()


def scatter_kernel(x_ref, f_ref, ox_ref, of_ref, lx, lf, sx, rx, sf, rf):
    x, y, z, c = coords()
    ctx, ch = peer(x, y, z, c)
    hub = ch * 128 + ctx
    own_x = pltpu.make_async_copy(x_ref.at[place(ctx, ch)], ox_ref.at[hub], lx)
    own_f = pltpu.make_async_copy(f_ref.at[ctx], of_ref.at[ctx], lf)
    own_x.start()
    own_f.start()

    def body(i, _):
        x2 = (x + i // 128) % 4
        y2 = (y + i // 2) % 8
        z2 = (z + i // 16) % 8
        c2 = (c + i) % 2
        ctx2, ch2 = peer(x2, y2, z2, c2)
        pltpu.make_async_remote_copy(
            x_ref.at[place(ctx2, ch2)], ox_ref.at[hub], sx, rx, device_id=(ctx2, ch2), device_id_type=MESH
        ).start()
        return 0

    lax.fori_loop(1, 512, body, 0)

    def body_f(i, _):
        ctx2 = (ctx + i) % 128
        pltpu.make_async_remote_copy(
            f_ref.at[ctx2], of_ref.at[ctx], sf, rf, device_id=(ctx2, ch), device_id_type=MESH
        ).start()
        return 0

    lax.fori_loop(1, 128, body_f, 0)
    own_x.wait()
    own_f.wait()
    for sem in (sx, rx):
        pltpu.make_async_copy(x_ref.at[pl.ds(0, 511)], ox_ref.at[pl.ds(0, 511)], sem).wait()
    for sem in (sf, rf):
        pltpu.make_async_copy(f_ref.at[pl.ds(0, 127)], of_ref.at[pl.ds(0, 127)], sem).wait()


def exchange(body, x, f, name):
    shapes = (jax.ShapeDtypeStruct((512, 4, 128), F32), jax.ShapeDtypeStruct((128, 2, 128), F32))
    ox, of = pl.pallas_call(
        body,
        out_shape=shapes,
        in_specs=[VM, VM],
        out_specs=(VM, VM),
        scratch_shapes=[pltpu.SemaphoreType.DMA] * 6,
        name=name,
        compiler_params=pltpu.CompilerParams(has_side_effects=True),
    )(x.reshape(512, 4, 128), f.reshape(128, 2, 128))
    return ox.reshape(2048, 128), of.reshape(256, 128)


def hub_kernel(r_ref, f_ref, o_ref, of_ref, pad, xl, il, ifw, y_acc, v_acc, phi, plo):
    ri = lax.broadcasted_iota(jnp.int32, (256, 256), 0)
    ci = lax.broadcasted_iota(jnp.int32, (256, 256), 1)
    flip = (ri + ci == 255).astype(F32).astype(BF)
    keep = lax.broadcasted_iota(jnp.int32, (128, 128), 1) >= lax.broadcasted_iota(jnp.int32, (128, 128), 0)
    early = lax.broadcasted_iota(jnp.int32, (128, 128), 1) <= lax.broadcasted_iota(jnp.int32, (128, 128), 0)
    lane_rev = 127 - lax.broadcasted_iota(jnp.int32, (256, 128), 1)
    for p in range(2):
        def load(s):
            return jnp.concatenate([r_ref[pl.ds(1024 * h + 2 * s + p, 256, stride=4), :] for h in range(2)], axis=1)
        x = load(0)
        g = load(1)
        g_low = g.astype(BF)
        g_rev = dot(g_low, flip)
        v_rev = dot(flip, x.astype(BF), 1, 1).astype(BF)
        pad[0:16, :] = jnp.zeros((16, 256), F32)
        pad[272:288, :] = jnp.zeros((16, 256), F32)
        pad[16:272, :] = x
        for m0 in range(4):
            sh = pad[16 - 4 * m0:272 - 4 * m0, :].astype(BF)
            xl[:, 256 * m0:256 * m0 + 128] = sh[:, 128:256]
            xl[:, 256 * m0 + 128:256 * m0 + 256] = sh[:, 0:128]
        pad[16:272, :] = g_rev
        for m0 in range(4):
            sh = pad[16 + 4 * m0:272 + 4 * m0, :].astype(BF)
            il[:, 256 * m0:256 * m0 + 128] = sh[:, 128:256]
            il[:, 256 * m0 + 128:256 * m0 + 256] = sh[:, 0:128]
        pad[16:272, :] = g
        for m0 in range(4):
            ifw[:, 256 * m0:256 * m0 + 256] = pad[16 + 4 * m0:272 + 4 * m0, :].astype(BF)
        phi[:, 0:128] = jnp.zeros((128, 128), BF)
        plo[:, 0:128] = jnp.zeros((128, 128), BF)
        prev = jnp.zeros((128, 128), F32)
        for u in range(128):
            row = jnp.broadcast_to(f_ref[pl.ds(2 * u + p, 1), :], (128, 128))
            turned = pltpu.roll(row, 0, 1, stride=1, stride_axis=0)
            band = jnp.where(keep, turned, prev)
            high = band.astype(BF)
            phi[:, 128 * (u + 1):128 * (u + 2)] = high
            plo[:, 128 * (u + 1):128 * (u + 2)] = (band - high.astype(F32)).astype(BF)
            prev = turned
        y_acc[...] = jnp.zeros((256, 256), F32)
        v_acc[...] = jnp.zeros((256, 256), F32)
        carry = jnp.zeros((128, 128), F32)
        before = jnp.zeros((128, 128), F32)
        for m1 in range(16):
            n = 256 - 16 * m1
            lhs = jnp.concatenate([xl[0:n, :], il[16 * m1:256, :]], axis=0)
            def slabs(ref):
                return jnp.concatenate([ref[:, 128 * k + 1024 * m1:128 * k + 1024 * m1 + 256] for k in range(8)], axis=0)
            res = dot(lhs, slabs(phi)) + dot(lhs, slabs(plo))
            y_acc[16 * m1:256, :] += res[0:n]
            v_acc[0:n, :] += res[n:]
            kk = n if n % 128 == 0 else (256 if n > 128 else 128)
            rhs = ifw[16 * m1:256, :]
            if kk > n:
                rhs = jnp.concatenate([rhs, jnp.zeros((kk - n, 1024), BF)], axis=0)
            z = dot(v_rev[:, 0:kk], rhs)
            for t in range(8):
                w = z[0:128, 128 * t:128 * t + 128]
                w = w + (carry if t == 0 else z[128:256, 128 * t - 128:128 * t])
                turned = pltpu.roll(w, 1, 1, stride=1, stride_axis=0)
                if 8 * m1 + t >= 2:
                    u = 8 * m1 + t - 2
                    of_ref[pl.ds(2 * u + p, 1), :] = jnp.sum(jnp.where(early, before, turned), axis=0, keepdims=True) * (1.0 / 256.0)
                before = turned
            carry = z[128:256, 896:1024]
        turned = pltpu.roll(carry, 1, 1, stride=1, stride_axis=0)
        of_ref[pl.ds(2 * 126 + p, 1), :] = jnp.sum(jnp.where(early, before, turned), axis=0, keepdims=True) * (1.0 / 256.0)
        of_ref[pl.ds(2 * 127 + p, 1), :] = jnp.sum(jnp.where(early, turned, 0.0), axis=0, keepdims=True) * (1.0 / 256.0)
        for h in range(2):
            o_ref[pl.ds(1024 * h + p, 256, stride=4), :] = y_acc[:, 128 * h:128 * h + 128]
            back = v_acc[:, 128 * (1 - h):128 * (1 - h) + 128]
            o_ref[pl.ds(1024 * h + 2 + p, 256, stride=4), :] = jnp.take_along_axis(back, lane_rev, axis=1)

def hub(r, f):
    vm = pl.BlockSpec(memory_space=pltpu.VMEM)
    return pl.pallas_call(hub_kernel,
        out_shape=(jax.ShapeDtypeStruct((2048, 128), F32), jax.ShapeDtypeStruct((256, 128), F32)),
        in_specs=[vm, vm], out_specs=(vm, vm), name="hub",
        scratch_shapes=[pltpu.VMEM((288, 256), F32), pltpu.VMEM((256, 1024), BF), pltpu.VMEM((256, 1024), BF), pltpu.VMEM((256, 1024), BF),
                        pltpu.VMEM((256, 256), F32), pltpu.VMEM((256, 256), F32), pltpu.VMEM((128, 16512), BF), pltpu.VMEM((128, 16512), BF)],
        compiler_params=pltpu.CompilerParams(vmem_limit_bytes=48 * 1024 * 1024))(r, f)

def unpack_kernel(b_ref, f_ref, grad_ref, gate_grad_ref, value_grad_ref, filter_grad_ref, wide):
    for p in range(2):
        wide[pl.ds(p, 512, stride=2), :] = b_ref[pl.ds(p, 512, stride=4), :]
    gate_grad_ref[...] = wide[...].T * grad_ref[...].astype(F32)
    for p in range(2):
        wide[pl.ds(p, 512, stride=2), :] = b_ref[pl.ds(2 + p, 512, stride=4), :]
    value_grad_ref[...] = wide[...].T
    filter_grad_ref[...] = f_ref[...].T


def per_device(gate_in, values, filters, out_grad):
    x, f = pl.pallas_call(
        pack_kernel,
        out_shape=(jax.ShapeDtypeStruct((2048, 128), F32), jax.ShapeDtypeStruct((256, 128), F32)),
        in_specs=[VM] * 4,
        out_specs=(VM, VM),
        scratch_shapes=[pltpu.VMEM((1024, 128), F32)],
        name="pack",
    )(gate_in, values, filters, out_grad)
    x, f = exchange(gather_kernel, x, f, "to_hubs")
    x, f = hub(x, f)
    x, f = exchange(scatter_kernel, x, f, "from_hubs")
    return pl.pallas_call(
        unpack_kernel,
        out_shape=(
            jax.ShapeDtypeStruct((128, 1024), F32),
            jax.ShapeDtypeStruct((128, 1024), F32),
            jax.ShapeDtypeStruct((128, 256), F32),
        ),
        in_specs=[VM] * 3,
        out_specs=(VM,) * 3,
        scratch_shapes=[pltpu.VMEM((1024, 128), F32)],
        name="unpack",
    )(x, f, out_grad)


def solution(mesh):
    return jax.shard_map(
        per_device,
        mesh=mesh,
        in_specs=(P("ctx", "ch"), P("ctx", "ch"), P("ctx", None), P("ctx", "ch")),
        out_specs=(P("ctx", "ch"), P("ctx", "ch"), P("ctx", "ch")),
        check_vma=False,
    )
```

time: 468 us -> 138 us (0.29); the launches traced: 459 us -> 137 us
  waiting for transfers between devices: 221 us -> 0 us
  Pallas kernels: 0 us -> 133 us
  local copies, waits for them, and re-layouts: 99.4 us -> 3.76 us
  starting transfers between devices: 88.5 us -> 0 us
  matrix products: 23.2 us -> 0 us
  between operations: 14.9 us -> 0.66 us
  other arithmetic: 12.9 us -> 0 us
    all_to_all x8 -> x0, waiting for transfers between devices: 218 us -> none  [the longest x2 82.6 us: inverse(): lax.all_to_all(back, 'ctx', split_axis=2, concat_axis=1, tiled=True)]
    pallas_call x0 -> x5, Pallas kernels: none -> 133 us  [the longest x2 111 us: exchange(): pl.pallas_call(body, out_shape=shapes, in_specs=[VM, VM], out_specs=(VM,...]
    all_to_all x8 -> x0, starting transfers between devices: 88.4 us -> none  [the longest x2 29.8 us: forward(): lax.all_to_all(stacked.reshape(members, 1, rows, cols), 'ctx', split_axis...]
    slice x10 -> x0, local copies, waits for them, and re-layouts: 31.8 us -> none  [the longest x2 17.1 us: inverse(): recv_re = arrived[0]]
    rev x4 -> x0, local copies, waits for them, and re-layouts: 25 us -> none  [the longest x2 15 us: mirror(): general = spectrum[::-1, ::-1]]
    dot_general x8 -> x0, matrix products: 23.2 us -> none  [the longest x2 7.85 us: forward(): spec = jnp.einsum('abkn,bfnc->afkc', inner_fwd, arrived, precision=highest)]
    another operation x3 -> x0, local copies, waits for them, and re-layouts: 9.25 us -> none  [the longest x2 6.99 us: forward(): jnp.stack([first[0] * twist_cos + first[1] * twist_sin, first[1] * twist_...]
    squeeze x5 -> x0, local copies, waits for them, and re-layouts: 8.27 us -> none  [the longest x2 3.73 us: inverse(): recv_im = arrived[1]]
  transfers between devices with their start and end apart: 9 -> 0, of which waited for: 9 -> 0; matrix products, arithmetic and copies ran while one was open for 18% -> 0% of each run, Pallas kernels for 0% -> 0%
where the time goes in v1:
time: 138 us; the launch traced here: 137 us
  Pallas kernels  133 us (96%)
  local copies, waits for them, and re-layouts  3.76 us (3%)
    pallas_call x2, Pallas kernels, exchange(): pl.pallas_call(body, out_shape=shapes, in_specs=[VM, VM], out_specs=(VM,...  111 us
    pallas_call x1, Pallas kernels, hub(): pl.pallas_call(hub_kernel, out_shape=(jax.ShapeDtypeStruct((2048, 128), F...  16.7 us
    unnamed x8, local copies, waits for them, and re-layouts  3.76 us

profile of v1, /device:TPU:1, one launch (start us, length us, event | category | flops | bytes accessed | tf_op | source)
XLA Modules:
  0.0 137.3 jit_solution(8444395139767614272)
XLA Ops:
  0.6 2.6 %pack.1 = (f32[2048,128]{1,0:T(8,128)}, f32[256,128]{1,0:T(8,128)}) custom-call(bf16[128,1024]{1,0:T(8,128)(2,1)} %gate_ref.1, bf16[128,1024]{1,0:T(8,128)(2,1)} %values_ref.1, f32[128,1024]{1,0:T(8,128)} %filters_ref.1, bf16[128,1024]{1,0:T(8,128)(2,1)} %grad_ref.3), custom_call_target="tpu_custom_call" | custom-call | tf_op jit(solution)/shard_map/pack/pallas_call | solution.py:229
  3.2 60.3 %to_hubs.1 = (f32[512,4,128]{2,1,0:T(4,128)}, f32[128,2,128]{2,1,0:T(2,128)}) custom-call(f32[512,4,128]{2,1,0:T(4,128)} %bitcast.12, f32[128,2,128]{2,1,0:T(2,128)} %bitcast.14), custom_call_target="tpu_custom_call" | custom-call | tf_op jit(solution)/shard_map/to_hubs/pallas_call | solution.py:122
  63.5 0.0 copy-start
  63.5 1.2 copy-done
  64.7 0.0 copy-start.2
  64.7 0.9 copy-done.2
  65.6 16.7 %hub.1 = (f32[2048,128]{1,0:T(8,128)S(1)}, f32[256,128]{1,0:T(8,128)S(1)}) custom-call(f32[2048,128]{1,0:T(8,128)S(1)} %bitcast.8, f32[256,128]{1,0:T(8,128)S(1)} %bitcast.10), custom_call_target="tpu_custom_call" | custom-call | tf_op jit(solution)/shard_map/hub/pallas_call | solution.py:211
  82.4 0.0 copy-start.1
  82.4 1.0 copy-done.1
  83.4 0.0 copy-start.3
  83.4 0.7 copy-done.3
  84.0 50.7 %from_hubs.1 = (f32[512,4,128]{2,1,0:T(4,128)}, f32[128,2,128]{2,1,0:T(2,128)}) custom-call(f32[512,4,128]{2,1,0:T(4,128)} %bitcast.9, f32[128,2,128]{2,1,0:T(2,128)} %bitcast.11), custom_call_target="tpu_custom_call" | custom-call | tf_op jit(solution)/shard_map/from_hubs/pallas_call | solution.py:122
  134.7 2.6 %unpack.1 = (f32[128,1024]{1,0:T(8,128)}, f32[128,1024]{1,0:T(8,128)}, f32[128,256]{1,0:T(8,128)}) custom-call(f32[2048,128]{1,0:T(8,128)} %bitcast.13, f32[256,128]{1,0:T(8,128)} %bitcast.15, bf16[128,1024]{1,0:T(8,128)(2,1)} %grad_ref.3), custom_call_target="tpu_custom_call" | custom-call | tf_op jit(solution)/shard_map/unpack/pallas_call | solution.py:240
Async XLA Ops:
  63.5 1.2 copy-start
  64.7 0.9 copy-start.2
  82.4 1.0 copy-start.1
  83.4 0.7 copy-start.3

commit v2 on v0

v2 whole, which is shorter than its diff:
```python
import functools

import jax
import jax.numpy as jnp
from jax import lax
from jax.experimental import pallas as pl
from jax.experimental.pallas import tpu as pltpu
from jax.sharding import PartitionSpec as P

BF = jnp.bfloat16
F32 = jnp.float32
MESH = pl.DeviceIdType.MESH
VM = pl.BlockSpec(memory_space=pltpu.VMEM)


def dot(a, b, ca=1, cb=0):
    return lax.dot_general(a, b, (((ca,), (cb,)), ((), ())), preferred_element_type=F32)


def flatten(x, y, zh, zl):
    ctx = zh * 32 + y * 4 + x
    return zl * 128 + ctx, lax.rem(ctx, 2) * 128 + lax.div(ctx, 2) * 2 + zl, ctx


def every_chip(visit):
    ctx = lax.axis_index("ctx")
    ch = lax.axis_index("ch")
    core = lax.rem(ch, 2)
    x = lax.rem(ctx, 4)
    y = lax.rem(lax.div(ctx, 4), 8)
    z = lax.div(ctx, 32) * 2 + lax.div(ch, 2)
    ys = [lax.rem(y + d, 8) for d in range(8)]

    def body(i, _):
        z2 = lax.rem(z + i, 8)
        x2 = lax.rem(x + lax.div(i, 8), 4)
        zh, zl = lax.div(z2, 2), lax.rem(z2, 2)
        for d in range(8):
            def one(y2=ys[d]):
                hub, place, ctx2 = flatten(x2, y2, zh, zl)
                visit(hub, place, ctx2, zl * 2 + core)
            if d == 0:
                pl.when(i > 0)(one)
            else:
                one()
        return 0

    lax.fori_loop(0, 32, body, 0)


def every_row(visit):
    ctx = lax.axis_index("ctx")

    def body(i, _):
        for k in range(8):
            def one(d=8 * i + k):
                visit(lax.rem(ctx + d, 128))
            if k == 0:
                pl.when(i > 0)(one)
            else:
                one()
        return 0

    lax.fori_loop(0, 16, body, 0)


def products(p, r_ref, f_ref, o_ref, of_ref, pad, xl, il, ifw, y_acc, v_acc, phi, plo):
    ri = lax.broadcasted_iota(jnp.int32, (256, 256), 0)
    ci = lax.broadcasted_iota(jnp.int32, (256, 256), 1)
    flip = (ri + ci == 255).astype(F32).astype(BF)
    row128 = lax.broadcasted_iota(jnp.int32, (128, 128), 0)
    lane128 = lax.broadcasted_iota(jnp.int32, (128, 128), 1)
    keep = lane128 >= row128
    early = lane128 <= row128
    lane_rev = 127 - lax.broadcasted_iota(jnp.int32, (256, 128), 1)

    def load(s):
        return jnp.concatenate(
            [r_ref[pl.ds(1024 * p + 512 * h + s, 256, stride=2), :] for h in range(2)], axis=1
        )

    x = load(0)
    g = load(1)
    g_rev = dot(g.astype(BF), flip)
    v_rev = dot(flip, x.astype(BF), 1, 1).astype(BF)
    pad[0:16, :] = jnp.zeros((16, 256), F32)
    pad[272:288, :] = jnp.zeros((16, 256), F32)
    pad[16:272, :] = x
    for m0 in range(4):
        sh = pad[16 - 4 * m0:272 - 4 * m0, :].astype(BF)
        xl[:, 256 * m0:256 * m0 + 128] = sh[:, 128:256]
        xl[:, 256 * m0 + 128:256 * m0 + 256] = sh[:, 0:128]
    pad[16:272, :] = g_rev
    for m0 in range(4):
        sh = pad[16 + 4 * m0:272 + 4 * m0, :].astype(BF)
        il[:, 256 * m0:256 * m0 + 128] = sh[:, 128:256]
        il[:, 256 * m0 + 128:256 * m0 + 256] = sh[:, 0:128]
    pad[16:272, :] = g
    for m0 in range(4):
        ifw[:, 256 * m0:256 * m0 + 256] = pad[16 + 4 * m0:272 + 4 * m0, :].astype(BF)
    phi[:, 0:128] = jnp.zeros((128, 128), BF)
    plo[:, 0:128] = jnp.zeros((128, 128), BF)
    prev = jnp.zeros((128, 128), F32)
    for u in range(128):
        row = jnp.broadcast_to(f_ref[pl.ds(2 * u + p, 1), :], (128, 128))
        turned = pltpu.roll(row, 0, 1, stride=1, stride_axis=0)
        band = jnp.where(keep, turned, prev)
        high = band.astype(BF)
        phi[:, 128 * (u + 1):128 * (u + 2)] = high
        plo[:, 128 * (u + 1):128 * (u + 2)] = (band - high.astype(F32)).astype(BF)
        prev = turned
    y_acc[...] = jnp.zeros((256, 256), F32)
    v_acc[...] = jnp.zeros((256, 256), F32)
    carry = jnp.zeros((128, 128), F32)
    before = jnp.zeros((128, 128), F32)

    def write(u, first, second):
        total = jnp.sum(jnp.where(early, first, second), axis=0, keepdims=True)
        of_ref[pl.ds(2 * u + p, 1), :] = total * (1.0 / 256.0)

    for m1 in range(16):
        n = 256 - 16 * m1
        lhs = jnp.concatenate([xl[0:n, :], il[16 * m1:256, :]], axis=0)

        def slabs(ref):
            return jnp.concatenate(
                [ref[:, 128 * k + 1024 * m1:128 * k + 1024 * m1 + 256] for k in range(8)], axis=0
            )

        res = dot(lhs, slabs(phi)) + dot(lhs, slabs(plo))
        y_acc[16 * m1:256, :] += res[0:n]
        v_acc[0:n, :] += res[n:]
        depth = 256 if n > 128 else 128
        rhs = ifw[16 * m1:256, :]
        if depth > n:
            rhs = jnp.concatenate([rhs, jnp.zeros((depth - n, 1024), BF)], axis=0)
        outer = dot(v_rev[:, 0:depth], rhs)
        for t in range(8):
            w = outer[0:128, 128 * t:128 * t + 128]
            w = w + (carry if t == 0 else outer[128:256, 128 * t - 128:128 * t])
            turned = pltpu.roll(w, 1, 1, stride=1, stride_axis=0)
            if 8 * m1 + t >= 2:
                write(8 * m1 + t - 2, before, turned)
            before = turned
        carry = outer[128:256, 896:1024]
    turned = pltpu.roll(carry, 1, 1, stride=1, stride_axis=0)
    write(126, before, turned)
    write(127, turned, jnp.zeros((128, 128), F32))
    for h in range(2):
        o_ref[pl.ds(1024 * p + 512 * h, 256, stride=2), :] = y_acc[:, 128 * h:128 * h + 128]
        back = v_acc[:, 128 * (1 - h):128 * (1 - h) + 128]
        o_ref[pl.ds(1024 * p + 512 * h + 1, 256, stride=2), :] = jnp.take_along_axis(back, lane_rev, axis=1)


SIB_IN, IN, FILT, OUT, GRAD, SIB_OUT = 0, 2, 4, 5, 7, 8


def main_kernel(
    gate_ref, values_ref, filters_ref, grad_ref, out_ref, ofg_ref,
    wide, mine, swap_in, xb, r, fb, hf, o, og, b, parts, swap_out,
    pad, xl, il, ifw, y_acc, v_acc, phi, plo, ssem, rsem, lsem,
):
    ctx = lax.axis_index("ctx")
    ch = lax.axis_index("ch")
    core = lax.rem(ch, 2)
    zl = lax.div(ch, 2)
    sibling = (ctx, zl * 2 + 1 - core)
    hub = zl * 128 + ctx
    place = lax.rem(ctx, 2) * 128 + lax.div(ctx, 2) * 2 + zl

    barrier = pltpu.get_barrier_semaphore()
    pl.semaphore_signal(barrier, inc=1, device_id=sibling, device_id_type=MESH)
    every_chip(
        lambda h2, p2, c2, ch2: pl.semaphore_signal(barrier, inc=1, device_id=(c2, ch2), device_id_type=MESH)
    )

    inner = (grad_ref[...].astype(F32) * gate_ref[...].astype(F32)).astype(BF)
    for s, signal in enumerate((values_ref[...], inner)):
        wide[...] = signal.astype(F32).T
        for c2 in range(2):
            for p in range(2):
                for z2 in range(2):
                    mine[c2, pl.ds((p * 256 + z2 * 128) * 2 + s, 128, stride=2), :] = (
                        wide[pl.ds(512 * z2 + 256 * c2 + p, 128, stride=2), :]
                    )
    fb[...] = filters_ref[:, pl.ds(pl.multiple_of(ch * 256, 256), 256)].T

    pl.semaphore_wait(barrier, 256)

    def send(src, dst, k, to):
        copy = pltpu.make_async_remote_copy(src, dst, ssem.at[k], rsem.at[k], device_id=to, device_id_type=MESH)
        copy.start()
        return copy

    def local(src, dst, k):
        copy = pltpu.make_async_copy(src, dst, lsem.at[k])
        copy.start()
        return copy

    def rows(ref, start, size):
        return ref.at[pl.ds(pl.multiple_of(start, size), size)]

    def landed(ref, count, k):
        pltpu.make_async_copy(ref.at[pl.ds(0, count)], ref.at[pl.ds(0, count)], rsem.at[k]).wait()

    def left(ref, count, k):
        pltpu.make_async_copy(ref.at[pl.ds(0, count)], ref.at[pl.ds(0, count)], ssem.at[k]).wait()

    swaps = [
        send(mine.at[1 - core, pl.ds(512 * p, 512)], swap_in.at[pl.ds(512 * p, 512)], SIB_IN + p, sibling)
        for p in range(2)
    ]
    own_f = local(rows(fb, 2 * ctx, 2), rows(hf, 2 * ctx, 2), 0)
    every_row(lambda c2: send(rows(fb, 2 * c2, 2), rows(hf, 2 * ctx, 2), FILT, (c2, ch)))
    own_in = []
    for p in range(2):
        swaps[p].wait_recv()
        for s in range(2):
            kept = mine[core, pl.ds(512 * p + s, 256, stride=2), :]
            got = swap_in[pl.ds(512 * p + s, 256, stride=2), :]
            xb[pl.ds(1024 * p + s, 256, stride=4), :] = jnp.where(core == 0, kept, got)
            xb[pl.ds(1024 * p + 2 + s, 256, stride=4), :] = jnp.where(core == 0, got, kept)
        own_in.append(local(rows(xb, 1024 * p + 4 * hub, 4), rows(r, 1024 * p + 4 * place, 4), 1 + p))
        every_chip(
            lambda h2, p2, c2, ch2: send(
                rows(xb, 1024 * p + 4 * h2, 4), rows(r, 1024 * p + 4 * place, 4), IN + p, (c2, ch2)
            )
        )
    own_out = []
    for p in range(2):
        own_in[p].wait()
        landed(r, 1020, IN + p)
        if p == 0:
            own_f.wait()
            landed(hf, 254, FILT)
        products(p, r, hf, o, og, pad, xl, il, ifw, y_acc, v_acc, phi, plo)
        own_out.append(local(rows(o, 1024 * p + 4 * place, 4), rows(b, 1024 * p + 4 * hub, 4), 3 + p))
        every_chip(
            lambda h2, p2, c2, ch2: send(
                rows(o, 1024 * p + 4 * p2, 4), rows(b, 1024 * p + 4 * hub, 4), OUT + p, (c2, ch2)
            )
        )
    own_g = local(rows(og, 2 * ctx, 2), rows(ofg_ref, 2 * ctx, 2), 5)
    every_row(lambda c2: send(rows(og, 2 * c2, 2), rows(ofg_ref, 2 * ctx, 2), GRAD, (c2, ch)))
    swaps_out = []
    for p in range(2):
        own_out[p].wait()
        landed(b, 1020, OUT + p)
        for s in range(2):
            for c2 in range(2):
                parts[c2, pl.ds(512 * p + s, 256, stride=2), :] = b[pl.ds(1024 * p + 2 * c2 + s, 256, stride=4), :]
        swaps_out.append(
            send(parts.at[1 - core, pl.ds(512 * p, 512)], swap_out.at[pl.ds(512 * p, 512)], SIB_OUT + p, sibling)
        )
    for p in range(2):
        swaps_out[p].wait_recv()
        for s in range(2):
            for z2 in range(2):
                at = pl.ds(512 * p + 256 * z2 + s, 128, stride=2)
                kept = parts[core, at, :]
                got = swap_out[at, :]
                out_ref[pl.ds(1024 * s + 512 * z2 + p, 128, stride=2), :] = jnp.where(core == 0, kept, got)
                out_ref[pl.ds(1024 * s + 512 * z2 + 256 + p, 128, stride=2), :] = jnp.where(core == 0, got, kept)
    own_g.wait()
    landed(ofg_ref, 254, GRAD)
    for p in range(2):
        swaps[p].wait_send()
        swaps_out[p].wait_send()
        left(xb, 1020, IN + p)
        left(o, 1020, OUT + p)
    left(fb, 254, FILT)
    left(og, 254, GRAD)


def unpack_kernel(b_ref, f_ref, grad_ref, gate_grad_ref, value_grad_ref, filter_grad_ref):
    gate_grad_ref[...] = b_ref[0:1024, :].T * grad_ref[...].astype(F32)
    value_grad_ref[...] = b_ref[1024:2048, :].T
    filter_grad_ref[...] = f_ref[...].T


def per_device(gate_in, values, filters, out_grad):
    def buf(rows, lanes=128, dtype=F32):
        return pltpu.VMEM((rows, lanes), dtype)

    out, fg = pl.pallas_call(
        main_kernel,
        out_shape=(jax.ShapeDtypeStruct((2048, 128), F32), jax.ShapeDtypeStruct((256, 128), F32)),
        in_specs=[VM] * 4,
        out_specs=(VM, VM),
        scratch_shapes=[
            buf(1024), pltpu.VMEM((2, 1024, 128), F32), buf(1024), buf(2048), buf(2048), buf(256), buf(256),
            buf(2048), buf(256), buf(2048), pltpu.VMEM((2, 1024, 128), F32), buf(1024),
            buf(288, 256), buf(256, 1024, BF), buf(256, 1024, BF), buf(256, 1024, BF),
            buf(256, 256), buf(256, 256), buf(128, 16512, BF), buf(128, 16512, BF),
            pltpu.SemaphoreType.DMA((10,)), pltpu.SemaphoreType.DMA((10,)), pltpu.SemaphoreType.DMA((6,)),
        ],
        name="through_hubs",
        compiler_params=pltpu.CompilerParams(
            collective_id=0, has_side_effects=True, vmem_limit_bytes=48 * 1024 * 1024
        ),
    )(gate_in, values, filters, out_grad)
    return pl.pallas_call(
        unpack_kernel,
        out_shape=(
            jax.ShapeDtypeStruct((128, 1024), F32),
            jax.ShapeDtypeStruct((128, 1024), F32),
            jax.ShapeDtypeStruct((128, 256), F32),
        ),
        in_specs=[VM] * 3,
        out_specs=(VM,) * 3,
        name="unpack",
    )(out, fg, out_grad)


def solution(mesh):
    return jax.shard_map(
        per_device,
        mesh=mesh,
        in_specs=(P("ctx", "ch"), P("ctx", "ch"), P("ctx", None), P("ctx", "ch")),
        out_specs=(P("ctx", "ch"), P("ctx", "ch"), P("ctx", "ch")),
        check_vma=False,
    )
```

time: 468 us -> 93.6 us (0.20); the launches traced: 459 us -> 93.3 us
  waiting for transfers between devices: 221 us -> 0 us
  local copies, waits for them, and re-layouts: 99.4 us -> 5.5 us
  starting transfers between devices: 88.5 us -> 0 us
  Pallas kernels: 0 us -> 87.1 us
  matrix products: 23.2 us -> 0 us
  between operations: 14.9 us -> 0.66 us
  other arithmetic: 12.9 us -> 0 us
    all_to_all x8 -> x0, waiting for transfers between devices: 218 us -> none  [the longest x2 82.6 us: inverse(): lax.all_to_all(back, 'ctx', split_axis=2, concat_axis=1, tiled=True)]
    all_to_all x8 -> x0, starting transfers between devices: 88.4 us -> none  [the longest x2 29.8 us: forward(): lax.all_to_all(stacked.reshape(members, 1, rows, cols), 'ctx', split_axis...]
    pallas_call x0 -> x2, Pallas kernels: none -> 87.1 us  [the longest x1 84.6 us: per_device(): pl.pallas_call(main_kernel, out_shape=(jax.ShapeDtypeStruct((2048, 128),...]
    slice x10 -> x0, local copies, waits for them, and re-layouts: 31.8 us -> none  [the longest x2 17.1 us: inverse(): recv_re = arrived[0]]
    rev x4 -> x0, local copies, waits for them, and re-layouts: 25 us -> none  [the longest x2 15 us: mirror(): general = spectrum[::-1, ::-1]]
    dot_general x8 -> x0, matrix products: 23.2 us -> none  [the longest x2 7.85 us: forward(): spec = jnp.einsum('abkn,bfnc->afkc', inner_fwd, arrived, precision=highest)]
    another operation x3 -> x0, local copies, waits for them, and re-layouts: 9.25 us -> none  [the longest x2 6.99 us: forward(): jnp.stack([first[0] * twist_cos + first[1] * twist_sin, first[1] * twist_...]
    squeeze x5 -> x0, local copies, waits for them, and re-layouts: 8.27 us -> none  [the longest x2 3.73 us: inverse(): recv_im = arrived[1]]
  transfers between devices with their start and end apart: 9 -> 0, of which waited for: 9 -> 0; matrix products, arithmetic and copies ran while one was open for 18% -> 0% of each run, Pallas kernels for 0% -> 0%
where the time goes in v2:
time: 93.6 us; the launch traced here: 93.3 us
  Pallas kernels  87.1 us (93%)
  local copies, waits for them, and re-layouts  5.5 us (6%)
    pallas_call x1, Pallas kernels, per_device(): pl.pallas_call(main_kernel, out_shape=(jax.ShapeDtypeStruct((2048, 128),...  84.6 us
    unnamed x12, local copies, waits for them, and re-layouts  5.5 us
    pallas_call x1, Pallas kernels, per_device(): pl.pallas_call(unpack_kernel, out_shape=(jax.ShapeDtypeStruct((128, 1024)...  2.54 us

profile of v2, /device:TPU:1, one launch (start us, length us, event | category | flops | bytes accessed | tf_op | source)
XLA Modules:
  0.0 93.3 jit_solution(11940968934526733671)
XLA Ops:
  0.6 0.0 copy-start.1
  0.6 0.9 %copy-done.1 = bf16[128,1024]{1,0:T(8,128)(2,1)S(1)} copy-done((bf16[128,1024]{1,0:T(8,128)(2,1)S(1)}, bf16[128,1024]{1,0:T(8,128)(2,1)}, u32[]{:S(2)}) %copy-start.1) | copy-done | bytes 262168
  1.6 0.0 copy-start.2
  1.6 1.0 %copy-done.2 = f32[128,1024]{1,0:T(8,128)S(1)} copy-done((f32[128,1024]{1,0:T(8,128)S(1)}, f32[128,1024]{1,0:T(8,128)}, u32[]{:S(2)}) %copy-start.2) | copy-done | bytes 524312
  2.6 0.0 copy-start.3
  2.6 0.9 %copy-done.3 = bf16[128,1024]{1,0:T(8,128)(2,1)S(1)} copy-done((bf16[128,1024]{1,0:T(8,128)(2,1)S(1)}, bf16[128,1024]{1,0:T(8,128)(2,1)}, u32[]{:S(2)}) %copy-start.3) | copy-done | bytes 262168
  3.6 0.0 copy-start.4
  3.6 0.9 %copy-done.4 = bf16[128,1024]{1,0:T(8,128)(2,1)S(1)} copy-done((bf16[128,1024]{1,0:T(8,128)(2,1)S(1)}, bf16[128,1024]{1,0:T(8,128)(2,1)}, u32[]{:S(2)}) %copy-start.4) | copy-done | bytes 262168
  4.5 84.6 %through_hubs.1 = (f32[2048,128]{1,0:T(8,128)S(1)}, f32[256,128]{1,0:T(8,128)S(1)}) custom-call(bf16[128,1024]{1,0:T(8,128)(2,1)S(1)} %copy-done.3, bf16[128,1024]{1,0:T(8,128)(2,1)S(1)} %copy-done.4, f32[128,1024]{1,0:T(8,128)S(1)} %copy-done.2, bf16[128,1024]{1,0:T(8,128)(2,1)S(1)} %copy-done.1), custom_call_target="tpu_custom_call" | custom-call | tf_op jit(solution)/shard_map/through_hubs/pallas_call | solution.py:285
  89.1 0.0 copy-start
  89.1 1.0 %copy-done = f32[2048,128]{1,0:T(8,128)} copy-done((f32[2048,128]{1,0:T(8,128)}, f32[2048,128]{1,0:T(8,128)S(1)}, u32[]{:S(2)}) %copy-start) | copy-done | bytes 1048600
  90.1 0.0 copy-start.5
  90.1 0.7 copy-done.5
  90.8 2.5 %unpack.1 = (f32[128,1024]{1,0:T(8,128)}, f32[128,1024]{1,0:T(8,128)}, f32[128,256]{1,0:T(8,128)}) custom-call(f32[2048,128]{1,0:T(8,128)} %copy-done, f32[256,128]{1,0:T(8,128)} %copy-done.5, bf16[128,1024]{1,0:T(8,128)(2,1)} %grad_ref.3), custom_call_target="tpu_custom_call" | custom-call | tf_op jit(solution)/shard_map/unpack/pallas_call | solution.py:302
Async XLA Ops:
  0.6 1.0 %copy-start.1 = (bf16[128,1024]{1,0:T(8,128)(2,1)S(1)}, bf16[128,1024]{1,0:T(8,128)(2,1)}, u32[]{:S(2)}) copy-start(bf16[128,1024]{1,0:T(8,128)(2,1)} %grad_ref.3) | copy-start | bytes 786436
  1.6 1.0 %copy-start.2 = (f32[128,1024]{1,0:T(8,128)S(1)}, f32[128,1024]{1,0:T(8,128)}, u32[]{:S(2)}) copy-start(f32[128,1024]{1,0:T(8,128)} %filters_ref.1) | copy-start | bytes 1572868
  2.6 0.9 %copy-start.3 = (bf16[128,1024]{1,0:T(8,128)(2,1)S(1)}, bf16[128,1024]{1,0:T(8,128)(2,1)}, u32[]{:S(2)}) copy-start(bf16[128,1024]{1,0:T(8,128)(2,1)} %gate_ref.1) | copy-start | bytes 786436
  3.6 0.9 %copy-start.4 = (bf16[128,1024]{1,0:T(8,128)(2,1)S(1)}, bf16[128,1024]{1,0:T(8,128)(2,1)}, u32[]{:S(2)}) copy-start(bf16[128,1024]{1,0:T(8,128)(2,1)} %values_ref.1) | copy-start | bytes 786436
  89.1 1.0 %copy-start = (f32[2048,128]{1,0:T(8,128)}, f32[2048,128]{1,0:T(8,128)S(1)}, u32[]{:S(2)}) copy-start(f32[2048,128]{1,0:T(8,128)S(1)} %get-tuple-element.5.b_ref) | copy-start | bytes 3145732
  90.1 0.7 copy-start.5

commit v3 on v2

v3 whole, which is shorter than its diff:
```python
import functools

import jax
import jax.numpy as jnp
from jax import lax
from jax.experimental import pallas as pl
from jax.experimental.pallas import tpu as pltpu
from jax.sharding import PartitionSpec as P

BF = jnp.bfloat16
F32 = jnp.float32
MESH = pl.DeviceIdType.MESH
VM = pl.BlockSpec(memory_space=pltpu.VMEM)


def dot(a, b, ca=1, cb=0):
    return lax.dot_general(a, b, (((ca,), (cb,)), ((), ())), preferred_element_type=F32)


def every_chip(visit):
    ctx = lax.axis_index("ctx")
    ch = lax.axis_index("ch")
    core = lax.rem(ch, 2)
    x = lax.rem(ctx, 4)
    y = lax.rem(lax.div(ctx, 4), 8)
    z = lax.div(ctx, 32) * 2 + lax.div(ch, 2)
    ys = [lax.rem(y + d, 8) * 4 for d in range(8)]
    zs = [lax.rem(z + d, 8) for d in range(8)]
    zls = [lax.rem(w, 2) for w in zs]
    zhs = [lax.div(w, 2) * 32 for w in zs]

    def body(i, _):
        x2 = lax.rem(x + i, 4)
        odd = lax.rem(x2, 2)
        shift = odd * 127
        for dz in range(8):
            for dy in range(8):
                def one(dz=dz, dy=dy):
                    ctx2 = zhs[dz] + ys[dy] + x2
                    visit(zls[dz] * 128 + ctx2, ctx2 + shift + zls[dz], ctx2, zls[dz] * 2 + core)
                if dz == 0 and dy == 0:
                    pl.when(i > 0)(one)
                else:
                    one()
        return 0

    lax.fori_loop(0, 4, body, 0)


def every_row(visit):
    ctx = lax.axis_index("ctx")

    def body(i, _):
        for k in range(8):
            def one(d=8 * i + k):
                visit(lax.rem(ctx + d, 128))
            if k == 0:
                pl.when(i > 0)(one)
            else:
                one()
        return 0

    lax.fori_loop(0, 16, body, 0)


def masks():
    row = lax.broadcasted_iota(jnp.int32, (128, 128), 0)
    lane = lax.broadcasted_iota(jnp.int32, (128, 128), 1)
    return row, lane


def flip_matrix():
    row = lax.broadcasted_iota(jnp.int32, (256, 256), 0)
    lane = lax.broadcasted_iota(jnp.int32, (256, 256), 1)
    return (row + lane == 255).astype(F32).astype(BF)


def bands(p, f_ref, phi, plo):
    row, lane = masks()
    keep = lane >= row
    phi[:, 0:128] = jnp.zeros((128, 128), BF)
    plo[:, 0:128] = jnp.zeros((128, 128), BF)
    prev = jnp.zeros((128, 128), F32)
    for u in range(128):
        taps = jnp.broadcast_to(f_ref[pl.ds(2 * u + p, 1), :], (128, 128))
        turned = pltpu.roll(taps, 0, 1, stride=1, stride_axis=0)
        band = jnp.where(keep, turned, prev)
        high = band.astype(BF)
        phi[:, 128 * (u + 1):128 * (u + 2)] = high
        plo[:, 128 * (u + 1):128 * (u + 2)] = (band - high.astype(F32)).astype(BF)
        prev = turned


def load_signal(p, s, r_ref):
    return jnp.concatenate(
        [r_ref[pl.ds(1024 * p + 512 * h + s, 256, stride=2), :] for h in range(2)], axis=1
    )


def convolve(p, r_ref, o_ref, pad, xl, il, y_acc, v_acc, phi, plo):
    pad[0:16, :] = jnp.zeros((16, 256), F32)
    pad[272:288, :] = jnp.zeros((16, 256), F32)
    pad[16:272, :] = load_signal(p, 0, r_ref)
    for m0 in range(4):
        sh = pad[16 - 4 * m0:272 - 4 * m0, :].astype(BF)
        xl[:, 256 * m0:256 * m0 + 128] = sh[:, 128:256]
        xl[:, 256 * m0 + 128:256 * m0 + 256] = sh[:, 0:128]
    pad[16:272, :] = dot(load_signal(p, 1, r_ref).astype(BF), flip_matrix())
    for m0 in range(4):
        sh = pad[16 + 4 * m0:272 + 4 * m0, :].astype(BF)
        il[:, 256 * m0:256 * m0 + 128] = sh[:, 128:256]
        il[:, 256 * m0 + 128:256 * m0 + 256] = sh[:, 0:128]
    y_acc[...] = jnp.zeros((256, 256), F32)
    v_acc[...] = jnp.zeros((256, 256), F32)
    for m1 in range(16):
        n = 256 - 16 * m1
        lhs = jnp.concatenate([xl[0:n, :], il[16 * m1:256, :]], axis=0)

        def slabs(ref):
            return jnp.concatenate(
                [ref[:, 128 * k + 1024 * m1:128 * k + 1024 * m1 + 256] for k in range(8)], axis=0
            )

        res = dot(lhs, slabs(phi)) + dot(lhs, slabs(plo))
        y_acc[16 * m1:256, :] += res[0:n]
        v_acc[0:n, :] += res[n:]
    lane_rev = 127 - lax.broadcasted_iota(jnp.int32, (256, 128), 1)
    for h in range(2):
        o_ref[pl.ds(1024 * p + 512 * h, 256, stride=2), :] = y_acc[:, 128 * h:128 * h + 128]
        back = v_acc[:, 128 * (1 - h):128 * (1 - h) + 128]
        o_ref[pl.ds(1024 * p + 512 * h + 1, 256, stride=2), :] = jnp.take_along_axis(back, lane_rev, axis=1)


def correlate(p, r_ref, of_ref, pad, ifw):
    row, lane = masks()
    early = lane <= row
    v_rev = dot(flip_matrix(), load_signal(p, 0, r_ref).astype(BF), 1, 1).astype(BF)
    pad[272:288, :] = jnp.zeros((16, 256), F32)
    pad[16:272, :] = load_signal(p, 1, r_ref)
    for m0 in range(4):
        ifw[:, 256 * m0:256 * m0 + 256] = pad[16 + 4 * m0:272 + 4 * m0, :].astype(BF)
    carry = jnp.zeros((128, 128), F32)
    before = jnp.zeros((128, 128), F32)

    def write(u, first, second):
        of_ref[pl.ds(2 * u + p, 1), :] = jnp.sum(jnp.where(early, first, second), axis=0, keepdims=True)

    for m1 in range(16):
        n = 256 - 16 * m1
        depth = 256 if n > 128 else 128
        rhs = ifw[16 * m1:256, :]
        if depth > n:
            rhs = jnp.concatenate([rhs, jnp.zeros((depth - n, 1024), BF)], axis=0)
        outer = dot(v_rev[:, 0:depth], rhs)
        for t in range(8):
            w = outer[0:128, 128 * t:128 * t + 128]
            w = w + (carry if t == 0 else outer[128:256, 128 * t - 128:128 * t])
            turned = pltpu.roll(w, 1, 1, stride=1, stride_axis=0)
            if 8 * m1 + t >= 2:
                write(8 * m1 + t - 2, before, turned)
            before = turned
        carry = outer[128:256, 896:1024]
    turned = pltpu.roll(carry, 1, 1, stride=1, stride_axis=0)
    write(126, before, turned)
    write(127, turned, jnp.zeros((128, 128), F32))


SIB_IN, IN, FILT, OUT, GRAD, SIB_OUT = 0, 2, 4, 5, 7, 8


def main_kernel(
    gate_ref, values_ref, filters_ref, grad_ref, gate_grad_ref, value_grad_ref, filter_grad_ref,
    gate_v, values_v, filters_v, grad_v,
    mine, swap_in, xb, r, fb, hf, o, og, b, fg, parts, swap_out,
    pad, xl, il, ifw, y_acc, v_acc, phi, plo, final, final_f, ssem, rsem, lsem,
):
    ctx = lax.axis_index("ctx")
    ch = lax.axis_index("ch")
    core = lax.rem(ch, 2)
    zl = lax.div(ch, 2)
    sibling = (ctx, zl * 2 + 1 - core)
    hub = zl * 128 + ctx
    place = lax.rem(ctx, 2) * 128 + lax.div(ctx, 2) * 2 + zl

    loads = [
        pltpu.make_async_copy(src, dst, lsem.at[6 + k])
        for k, (src, dst) in enumerate((
            (values_ref, values_v), (gate_ref, gate_v), (grad_ref, grad_v),
            (filters_ref.at[:, pl.ds(pl.multiple_of(ch * 256, 256), 256)], filters_v),
        ))
    ]
    for copy in loads:
        copy.start()
    barrier = pltpu.get_barrier_semaphore()
    pl.semaphore_signal(barrier, inc=1, device_id=sibling, device_id_type=MESH)
    every_chip(
        lambda h2, p2, c2, ch2: pl.semaphore_signal(barrier, inc=1, device_id=(c2, ch2), device_id_type=MESH)
    )
    for copy in loads:
        copy.wait()

    def pack(p):
        for z2 in range(2):
            for c2 in range(2):
                lanes = slice(512 * z2 + 256 * c2 + 128 * p, 512 * z2 + 256 * c2 + 128 * p + 128)
                inner = (grad_v[:, lanes].astype(F32) * gate_v[:, lanes].astype(F32)).astype(BF)
                for s, signal in enumerate((values_v[:, lanes], inner)):
                    mine[c2, pl.ds((p * 256 + z2 * 128) * 2 + s, 128, stride=2), :] = signal.astype(F32).T

    for p in range(2):
        fb[pl.ds(p, 128, stride=2), :] = filters_v[:, 128 * p:128 * p + 128].T
    pack(0)

    pl.semaphore_wait(barrier, 256)

    def send(src, dst, k, to):
        copy = pltpu.make_async_remote_copy(src, dst, ssem.at[k], rsem.at[k], device_id=to, device_id_type=MESH)
        copy.start()
        return copy

    def local(src, dst, k):
        copy = pltpu.make_async_copy(src, dst, lsem.at[k])
        copy.start()
        return copy

    def rows(ref, start, size):
        return ref.at[pl.ds(pl.multiple_of(start, size), size)]

    def landed(ref, count, k):
        pltpu.make_async_copy(ref.at[pl.ds(0, count)], ref.at[pl.ds(0, count)], rsem.at[k]).wait()

    def left(ref, count, k):
        pltpu.make_async_copy(ref.at[pl.ds(0, count)], ref.at[pl.ds(0, count)], ssem.at[k]).wait()

    def swap(p):
        return send(mine.at[1 - core, pl.ds(512 * p, 512)], swap_in.at[pl.ds(512 * p, 512)], SIB_IN + p, sibling)

    swaps = [swap(0)]
    own_f = local(rows(fb, 2 * ctx, 2), rows(hf, 2 * ctx, 2), 0)
    every_row(lambda c2: send(rows(fb, 2 * c2, 2), rows(hf, 2 * ctx, 2), FILT, (c2, ch)))
    pack(1)
    swaps.append(swap(1))
    own_in = []
    for p in range(2):
        swaps[p].wait_recv()
        for s in range(2):
            kept = mine[core, pl.ds(512 * p + s, 256, stride=2), :]
            got = swap_in[pl.ds(512 * p + s, 256, stride=2), :]
            xb[pl.ds(1024 * p + s, 256, stride=4), :] = jnp.where(core == 0, kept, got)
            xb[pl.ds(1024 * p + 2 + s, 256, stride=4), :] = jnp.where(core == 0, got, kept)
        own_in.append(local(rows(xb, 1024 * p + 4 * hub, 4), rows(r, 1024 * p + 4 * place, 4), 1 + p))
        every_chip(
            lambda h2, p2, c2, ch2: send(
                rows(xb, 1024 * p + 4 * h2, 4), rows(r, 1024 * p + 4 * place, 4), IN + p, (c2, ch2)
            )
        )
    own_f.wait()
    landed(hf, 254, FILT)
    for p in range(2):
        bands(p, hf, phi.at[p], plo.at[p])
    own_out = []
    for p in range(2):
        own_in[p].wait()
        landed(r, 1020, IN + p)
        convolve(p, r, o, pad, xl, il, y_acc, v_acc, phi.at[p], plo.at[p])
        own_out.append(local(rows(o, 1024 * p + 4 * place, 4), rows(b, 1024 * p + 4 * hub, 4), 3 + p))
        every_chip(
            lambda h2, p2, c2, ch2: send(
                rows(o, 1024 * p + 4 * p2, 4), rows(b, 1024 * p + 4 * hub, 4), OUT + p, (c2, ch2)
            )
        )
        correlate(p, r, og, pad, ifw)
    stores = []
    own_g = local(rows(og, 2 * ctx, 2), rows(fg, 2 * ctx, 2), 5)
    every_row(lambda c2: send(rows(og, 2 * c2, 2), rows(fg, 2 * ctx, 2), GRAD, (c2, ch)))
    for p in range(2):
        own_out[p].wait()
        landed(b, 1020, OUT + p)
        for s in range(2):
            for c2 in range(2):
                parts[c2, pl.ds(512 * p + s, 256, stride=2), :] = b[pl.ds(1024 * p + 2 * c2 + s, 256, stride=4), :]
        back = send(parts.at[1 - core, pl.ds(512 * p, 512)], swap_out.at[pl.ds(512 * p, 512)], SIB_OUT + p, sibling)
        back.wait_recv()
        for z2 in range(2):
            for s in range(2):
                at = pl.ds(512 * p + 256 * z2 + s, 128, stride=2)
                kept = parts[core, at, :]
                got = swap_out[at, :]
                lane = 512 * z2 + 128 * p
                first = jnp.where(core == 0, kept, got).T
                second = jnp.where(core == 0, got, kept).T
                if s == 0:
                    first = first * grad_v[:, lane:lane + 128].astype(F32)
                    second = second * grad_v[:, lane + 256:lane + 384].astype(F32)
                final[s, :, lane:lane + 128] = first
                final[s, :, lane + 256:lane + 384] = second
                for c2 in range(2):
                    lanes = pl.ds(lane + 256 * c2, 128)
                    stores.append(local(final.at[s, :, lanes], (gate_grad_ref, value_grad_ref)[s].at[:, lanes], 10 + len(stores)))
        back.wait_send()
    own_g.wait()
    landed(fg, 254, GRAD)
    for p in range(2):
        final_f[:, 128 * p:128 * p + 128] = fg[pl.ds(p, 128, stride=2), :].T * (1.0 / 256.0)
    stores.append(local(final_f, filter_grad_ref, 10 + len(stores)))
    for p in range(2):
        swaps[p].wait_send()
        left(xb, 1020, IN + p)
        left(o, 1020, OUT + p)
    left(fb, 254, FILT)
    left(og, 254, GRAD)
    for copy in stores:
        copy.wait()


def hand_over_kernel(a_ref, b_ref, c_ref, oa_ref, ob_ref, oc_ref, sem):
    copies = [
        pltpu.make_async_copy(src, dst, sem.at[k])
        for k, (src, dst) in enumerate(((a_ref, oa_ref), (b_ref, ob_ref), (c_ref, oc_ref)))
    ]
    for copy in copies:
        copy.start()
    for copy in copies:
        copy.wait()


def per_device(gate_in, values, filters, out_grad):
    def buf(rows, lanes=128, dtype=F32):
        return pltpu.VMEM((rows, lanes), dtype)

    anywhere = pl.BlockSpec(memory_space=pltpu.HBM)
    shapes = (
        jax.ShapeDtypeStruct((128, 1024), F32),
        jax.ShapeDtypeStruct((128, 1024), F32),
        jax.ShapeDtypeStruct((128, 256), F32),
    )
    results = pl.pallas_call(
        main_kernel,
        out_shape=shapes,
        in_specs=[anywhere] * 4,
        out_specs=(anywhere,) * 3,
        scratch_shapes=[
            buf(128, 1024, BF), buf(128, 1024, BF), buf(128, 256), buf(128, 1024, BF),
            pltpu.VMEM((2, 1024, 128), F32), buf(1024), buf(2048), buf(2048), buf(256), buf(256),
            buf(2048), buf(256), buf(2048), buf(256), pltpu.VMEM((2, 1024, 128), F32), buf(1024),
            buf(288, 256), buf(256, 1024, BF), buf(256, 1024, BF), buf(256, 1024, BF),
            buf(256, 256), buf(256, 256), pltpu.VMEM((2, 128, 16512), BF), pltpu.VMEM((2, 128, 16512), BF),
            pltpu.VMEM((2, 128, 1024), F32), buf(128, 256),
            pltpu.SemaphoreType.DMA((10,)), pltpu.SemaphoreType.DMA((10,)), pltpu.SemaphoreType.DMA((27,)),
        ],
        name="through_hubs",
        compiler_params=pltpu.CompilerParams(
            collective_id=0, has_side_effects=True, vmem_limit_bytes=62 * 1024 * 1024
        ),
    )(gate_in, values, filters, out_grad)
    return pl.pallas_call(
        hand_over_kernel,
        out_shape=shapes,
        in_specs=[anywhere] * 3,
        out_specs=(anywhere,) * 3,
        scratch_shapes=[pltpu.SemaphoreType.DMA((3,))],
        name="hand_over",
        compiler_params=pltpu.CompilerParams(vmem_limit_bytes=62 * 1024 * 1024),
    )(*results)


def solution(mesh):
    return jax.shard_map(
        per_device,
        mesh=mesh,
        in_specs=(P("ctx", "ch"), P("ctx", "ch"), P("ctx", None), P("ctx", "ch")),
        out_specs=(P("ctx", "ch"), P("ctx", "ch"), P("ctx", "ch")),
        check_vma=False,
    )
```

time: 93.6 us -> 124 us (1.32)
  Pallas kernels: 87.1 us -> 123 us
  local copies, waits for them, and re-layouts: 5.5 us -> 0 us
    pallas_call x2, Pallas kernels: 87.1 us -> 123 us  [the longest x1 86.6 us: per_device(): pl.pallas_call(main_kernel, out_shape=shapes, in_specs=[anywhere] * 4, ou...]
    unnamed x12 -> x0, local copies, waits for them, and re-layouts: 5.5 us -> none
where the time goes in v3:
time: 124 us
  Pallas kernels  123 us (99%)
    pallas_call x1, Pallas kernels, per_device(): pl.pallas_call(main_kernel, out_shape=shapes, in_specs=[anywhere] * 4, ou...  86.6 us
    pallas_call x1, Pallas kernels, per_device(): pl.pallas_call(hand_over_kernel, out_shape=shapes, in_specs=[anywhere] *...  36.9 us

profile of v3, /device:TPU:1, one launch (start us, length us, event | category | flops | bytes accessed | tf_op | source)
XLA Modules:
  0.0 124.3 jit_solution(4430810728685993827)
XLA Ops:
  0.6 86.6 %through_hubs.1 = (f32[128,1024]{1,0:T(8,128)}, f32[128,1024]{1,0:T(8,128)}, f32[128,256]{1,0:T(8,128)}) custom-call(bf16[128,1024]{1,0:T(8,128)(2,1)} %gate_ref.1, bf16[128,1024]{1,0:T(8,128)(2,1)} %values_ref.1, f32[128,1024]{1,0:T(8,128)} %filters_ref.1, bf16[128,1024]{1,0:T(8,128)(2,1)} %grad_ref.1), custom_call_target="tpu_custom_call" | custom-call | tf_op jit(solution)/shard_map/through_hubs/pallas_call | solution.py:337
  87.2 36.9 %hand_over.1 = (f32[128,1024]{1,0:T(8,128)}, f32[128,1024]{1,0:T(8,128)}, f32[128,256]{1,0:T(8,128)}) custom-call(f32[128,1024]{1,0:T(8,128)} %get-tuple-element.6.a_ref, f32[128,1024]{1,0:T(8,128)} %get-tuple-element.7.b_ref, f32[128,256]{1,0:T(8,128)} %get-tuple-element.8.c_ref), custom_call_target="tpu_custom_call" | custom-call | tf_op jit(solution)/shard_map/hand_over/pallas_call | solution.py:356

commit v4 on v2

--- a/solution.py
+++ b/solution.py
@@ -15,11 +15,6 @@
 
 def dot(a, b, ca=1, cb=0):
     return lax.dot_general(a, b, (((ca,), (cb,)), ((), ())), preferred_element_type=F32)
-
-
-def flatten(x, y, zh, zl):
-    ctx = zh * 32 + y * 4 + x
-    return zl * 128 + ctx, lax.rem(ctx, 2) * 128 + lax.div(ctx, 2) * 2 + zl, ctx
 
 
 def every_chip(visit):
@@ -29,23 +24,27 @@
     x = lax.rem(ctx, 4)
     y = lax.rem(lax.div(ctx, 4), 8)
     z = lax.div(ctx, 32) * 2 + lax.div(ch, 2)
-    ys = [lax.rem(y + d, 8) for d in range(8)]
+    ys = [lax.rem(y + d, 8) * 4 for d in range(8)]
+    zs = [lax.rem(z + d, 8) for d in range(8)]
+    zls = [lax.rem(w, 2) for w in zs]
+    zhs = [lax.div(w, 2) * 32 for w in zs]
 
     def body(i, _):
-        z2 = lax.rem(z + i, 8)
-        x2 = lax.rem(x + lax.div(i, 8), 4)
-        zh, zl = lax.div(z2, 2), lax.rem(z2, 2)
-        for d in range(8):
-            def one(y2=ys[d]):
-                hub, place, ctx2 = flatten(x2, y2, zh, zl)
-                visit(hub, place, ctx2, zl * 2 + core)
-            if d == 0:
-                pl.when(i > 0)(one)
-            else:
-                one()
+        x2 = lax.rem(x + i, 4)
+        odd = lax.rem(x2, 2)
+        shift = odd * 127
+        for dz in range(8):
+            for dy in range(8):
+                def one(dz=dz, dy=dy):
+                    ctx2 = zhs[dz] + ys[dy] + x2
+                    visit(zls[dz] * 128 + ctx2, ctx2 + shift + zls[dz], ctx2, zls[dz] * 2 + core)
+                if dz == 0 and dy == 0:
+                    pl.when(i > 0)(one)
+                else:
+                    one()
         return 0
 
-    lax.fori_loop(0, 32, body, 0)
+    lax.fori_loop(0, 4, body, 0)
 
 
 def every_row(visit):
@@ -116,7 +115,7 @@
 
     def write(u, first, second):
         total = jnp.sum(jnp.where(early, first, second), axis=0, keepdims=True)
-        of_ref[pl.ds(2 * u + p, 1), :] = total * (1.0 / 256.0)
+        of_ref[pl.ds(2 * u + p, 1), :] = total
 
     for m1 in range(16):
         n = 256 - 16 * m1
@@ -156,8 +155,9 @@
 
 
 def main_kernel(
-    gate_ref, values_ref, filters_ref, grad_ref, out_ref, ofg_ref,
-    wide, mine, swap_in, xb, r, fb, hf, o, og, b, parts, swap_out,
+    gate_ref, values_ref, filters_ref, grad_ref, conv_ref, back_ref, fgrad_ref,
+    gate_v, values_v, filters_v, grad_v,
+    mine, swap_in, xb, r, fb, hf, o, og, b, fg, parts, swap_out,
     pad, xl, il, ifw, y_acc, v_acc, phi, plo, ssem, rsem, lsem,
 ):
     ctx = lax.axis_index("ctx")
@@ -168,22 +168,34 @@
     hub = zl * 128 + ctx
     place = lax.rem(ctx, 2) * 128 + lax.div(ctx, 2) * 2 + zl
 
+    loads = [
+        pltpu.make_async_copy(src, dst, lsem.at[6 + k])
+        for k, (src, dst) in enumerate((
+            (values_ref, values_v), (gate_ref, gate_v), (grad_ref, grad_v),
+            (filters_ref.at[:, pl.ds(pl.multiple_of(ch * 256, 256), 256)], filters_v),
+        ))
+    ]
+    for copy in loads:
+        copy.start()
     barrier = pltpu.get_barrier_semaphore()
     pl.semaphore_signal(barrier, inc=1, device_id=sibling, device_id_type=MESH)
     every_chip(
         lambda h2, p2, c2, ch2: pl.semaphore_signal(barrier, inc=1, device_id=(c2, ch2), device_id_type=MESH)
     )
-
-    inner = (grad_ref[...].astype(F32) * gate_ref[...].astype(F32)).astype(BF)
-    for s, signal in enumerate((values_ref[...], inner)):
-        wide[...] = signal.astype(F32).T
-        for c2 in range(2):
-            for p in range(2):
-                for z2 in range(2):
-                    mine[c2, pl.ds((p * 256 + z2 * 128) * 2 + s, 128, stride=2), :] = (
-                        wide[pl.ds(512 * z2 + 256 * c2 + p, 128, stride=2), :]
-                    )
-    fb[...] = filters_ref[:, pl.ds(pl.multiple_of(ch * 256, 256), 256)].T
+    for copy in loads:
+        copy.wait()
+
+    def pack(p):
+        for z2 in range(2):
+            for c2 in range(2):
+                lanes = slice(512 * z2 + 256 * c2 + 128 * p, 512 * z2 + 256 * c2 + 128 * p + 128)
+                inner = (grad_v[:, lanes].astype(F32) * gate_v[:, lanes].astype(F32)).astype(BF)
+                for s, signal in enumerate((values_v[:, lanes], inner)):
+                    mine[c2, pl.ds((p * 256 + z2 * 128) * 2 + s, 128, stride=2), :] = signal.astype(F32).T
+
+    for p in range(2):
+        fb[pl.ds(p, 128, stride=2), :] = filters_v[:, 128 * p:128 * p + 128].T
+    pack(0)
 
     pl.semaphore_wait(barrier, 256)
 
@@ -206,12 +218,14 @@
     def left(ref, count, k):
         pltpu.make_async_copy(ref.at[pl.ds(0, count)], ref.at[pl.ds(0, count)], ssem.at[k]).wait()
 
-    swaps = [
-        send(mine.at[1 - core, pl.ds(512 * p, 512)], swap_in.at[pl.ds(512 * p, 512)], SIB_IN + p, sibling)
-        for p in range(2)
-    ]
+    def swap(p):
+        return send(mine.at[1 - core, pl.ds(512 * p, 512)], swap_in.at[pl.ds(512 * p, 512)], SIB_IN + p, sibling)
+
+    swaps = [swap(0)]
     own_f = local(rows(fb, 2 * ctx, 2), rows(hf, 2 * ctx, 2), 0)
     every_row(lambda c2: send(rows(fb, 2 * c2, 2), rows(hf, 2 * ctx, 2), FILT, (c2, ch)))
+    pack(1)
+    swaps.append(swap(1))
     own_in = []
     for p in range(2):
         swaps[p].wait_recv()
@@ -240,76 +254,65 @@
                 rows(o, 1024 * p + 4 * p2, 4), rows(b, 1024 * p + 4 * hub, 4), OUT + p, (c2, ch2)
             )
         )
-    own_g = local(rows(og, 2 * ctx, 2), rows(ofg_ref, 2 * ctx, 2), 5)
-    every_row(lambda c2: send(rows(og, 2 * c2, 2), rows(ofg_ref, 2 * ctx, 2), GRAD, (c2, ch)))
-    swaps_out = []
+    own_g = local(rows(og, 2 * ctx, 2), rows(fg, 2 * ctx, 2), 5)
+    every_row(lambda c2: send(rows(og, 2 * c2, 2), rows(fg, 2 * ctx, 2), GRAD, (c2, ch)))
     for p in range(2):
         own_out[p].wait()
         landed(b, 1020, OUT + p)
         for s in range(2):
             for c2 in range(2):
                 parts[c2, pl.ds(512 * p + s, 256, stride=2), :] = b[pl.ds(1024 * p + 2 * c2 + s, 256, stride=4), :]
-        swaps_out.append(
-            send(parts.at[1 - core, pl.ds(512 * p, 512)], swap_out.at[pl.ds(512 * p, 512)], SIB_OUT + p, sibling)
-        )
-    for p in range(2):
-        swaps_out[p].wait_recv()
-        for s in range(2):
+        back = send(parts.at[1 - core, pl.ds(512 * p, 512)], swap_out.at[pl.ds(512 * p, 512)], SIB_OUT + p, sibling)
+        back.wait_recv()
+        for s, out in enumerate((conv_ref, back_ref)):
             for z2 in range(2):
                 at = pl.ds(512 * p + 256 * z2 + s, 128, stride=2)
                 kept = parts[core, at, :]
                 got = swap_out[at, :]
-                out_ref[pl.ds(1024 * s + 512 * z2 + p, 128, stride=2), :] = jnp.where(core == 0, kept, got)
-                out_ref[pl.ds(1024 * s + 512 * z2 + 256 + p, 128, stride=2), :] = jnp.where(core == 0, got, kept)
+                lane = 512 * z2 + 128 * p
+                out[:, lane:lane + 128] = jnp.where(core == 0, kept, got).T
+                out[:, lane + 256:lane + 384] = jnp.where(core == 0, got, kept).T
+        back.wait_send()
     own_g.wait()
-    landed(ofg_ref, 254, GRAD)
+    landed(fg, 254, GRAD)
+    for p in range(2):
+        fgrad_ref[:, 128 * p:128 * p + 128] = fg[pl.ds(p, 128, stride=2), :].T
     for p in range(2):
         swaps[p].wait_send()
-        swaps_out[p].wait_send()
         left(xb, 1020, IN + p)
         left(o, 1020, OUT + p)
     left(fb, 254, FILT)
     left(og, 254, GRAD)
 
 
-def unpack_kernel(b_ref, f_ref, grad_ref, gate_grad_ref, value_grad_ref, filter_grad_ref):
-    gate_grad_ref[...] = b_ref[0:1024, :].T * grad_ref[...].astype(F32)
-    value_grad_ref[...] = b_ref[1024:2048, :].T
-    filter_grad_ref[...] = f_ref[...].T
-
-
 def per_device(gate_in, values, filters, out_grad):
     def buf(rows, lanes=128, dtype=F32):
         return pltpu.VMEM((rows, lanes), dtype)
 
-    out, fg = pl.pallas_call(
+    anywhere = pl.BlockSpec(memory_space=pltpu.HBM)
+    conv, back, fg = pl.pallas_call(
         main_kernel,
-        out_shape=(jax.ShapeDtypeStruct((2048, 128), F32), jax.ShapeDtypeStruct((256, 128), F32)),
-        in_specs=[VM] * 4,
-        out_specs=(VM, VM),
-        scratch_shapes=[
-            buf(1024), pltpu.VMEM((2, 1024, 128), F32), buf(1024), buf(2048), buf(2048), buf(256), buf(256),
-            buf(2048), buf(256), buf(2048), pltpu.VMEM((2, 1024, 128), F32), buf(1024),
-            buf(288, 256), buf(256, 1024, BF), buf(256, 1024, BF), buf(256, 1024, BF),
-            buf(256, 256), buf(256, 256), buf(128, 16512, BF), buf(128, 16512, BF),
-            pltpu.SemaphoreType.DMA((10,)), pltpu.SemaphoreType.DMA((10,)), pltpu.SemaphoreType.DMA((6,)),
-        ],
-        name="through_hubs",
-        compiler_params=pltpu.CompilerParams(
-            collective_id=0, has_side_effects=True, vmem_limit_bytes=48 * 1024 * 1024
-        ),
-    )(gate_in, values, filters, out_grad)
-    return pl.pallas_call(
-        unpack_kernel,
         out_shape=(
             jax.ShapeDtypeStruct((128, 1024), F32),
             jax.ShapeDtypeStruct((128, 1024), F32),
             jax.ShapeDtypeStruct((128, 256), F32),
         ),
-        in_specs=[VM] * 3,
+        in_specs=[anywhere] * 4,
         out_specs=(VM,) * 3,
-        name="unpack",
-    )(out, fg, out_grad)
+        scratch_shapes=[
+            buf(128, 1024, BF), buf(128, 1024, BF), buf(128, 256), buf(128, 1024, BF),
+            pltpu.VMEM((2, 1024, 128), F32), buf(1024), buf(2048), buf(2048), buf(256), buf(256),
+            buf(2048), buf(256), buf(2048), buf(256), pltpu.VMEM((2, 1024, 128), F32), buf(1024),
+            buf(288, 256), buf(256, 1024, BF), buf(256, 1024, BF), buf(256, 1024, BF),
+            buf(256, 256), buf(256, 256), buf(128, 16512, BF), buf(128, 16512, BF),
+            pltpu.SemaphoreType.DMA((10,)), pltpu.SemaphoreType.DMA((10,)), pltpu.SemaphoreType.DMA((10,)),
+        ],
+        name="through_hubs",
+        compiler_params=pltpu.CompilerParams(
+            collective_id=0, has_side_effects=True, vmem_limit_bytes=62 * 1024 * 1024
+        ),
+    )(gate_in, values, filters, out_grad)
+    return out_grad.astype(F32) * conv, back, fg * (1.0 / 256.0)
 
 
 def solution(mesh):

time: 93.6 us -> 87.8 us (0.938)
  local copies, waits for them, and re-layouts: 5.5 us -> 0.81 us
  Pallas kernels: 87.1 us -> 83.6 us
  other arithmetic: 0 us -> 2.62 us
    unnamed x12 -> x7, local copies, waits for them, and re-layouts: 5.5 us -> 0.81 us
    pallas_call x2 -> x1, Pallas kernels: 87.1 us -> 83.6 us  [per_device(): pl.pallas_call(main_kernel, out_shape=(jax.ShapeDtypeStruct((128, 1024),...]
    mul x0 -> x2, other arithmetic: none -> 2.62 us  [per_device(): return (out_grad.astype(F32) * conv, back, fg * (1.0 / 256.0))]
where the time goes in v4:
time: 87.8 us; the launch traced here: 87.7 us
  Pallas kernels  83.6 us (95%)
  other arithmetic  2.62 us (3%)
    pallas_call x1, Pallas kernels, per_device(): pl.pallas_call(main_kernel, out_shape=(jax.ShapeDtypeStruct((128, 1024),...  83.6 us
    mul x2, other arithmetic, per_device(): return (out_grad.astype(F32) * conv, back, fg * (1.0 / 256.0))  2.62 us

profile of v4, /device:TPU:1, one launch (start us, length us, event | category | flops | bytes accessed | tf_op | source)
XLA Modules:
  0.0 87.7 jit_solution(9016953496694427383)
XLA Ops:
  0.6 0.0 copy-start
  0.6 83.6 %through_hubs.1 = (f32[128,1024]{1,0:T(8,128)}, f32[128,1024]{1,0:T(8,128)}, f32[128,256]{1,0:T(8,128)}) custom-call(bf16[128,1024]{1,0:T(8,128)(2,1)} %gate_ref.1, bf16[128,1024]{1,0:T(8,128)(2,1)} %values_ref.1, f32[128,1024]{1,0:T(8,128)} %filters_ref.1, bf16[128,1024]{1,0:T(8,128)(2,1)} %grad_ref.1), custom_call_target="tpu_custom_call" | custom-call | tf_op jit(solution)/shard_map/through_hubs/pallas_call | solution.py:293
  84.2 0.0 copy-done
  84.2 0.0 copy-start.2
  84.2 0.0 copy-start.1
  84.2 2.0 %convert_multiply_fusion = f32[128,1024]{1,0:T(8,128)} fusion(f32[128,1024]{1,0:T(8,128)} %get-tuple-element.6, bf16[128,1024]{1,0:T(8,128)(2,1)S(1)} %copy-done), kind=kLoop, calls=%fused_computation | loop fusion | flops 262144 | bytes 1310720 | tf_op jit(solution)/shard_map/mul | solution.py:315
  86.2 0.0 copy-done.2
  86.2 0.7 broadcast_multiply_fusion
  86.9 0.0 copy-done.1
  86.9 0.8 copy.8
Async XLA Ops:
  0.6 83.6 %copy-start = (bf16[128,1024]{1,0:T(8,128)(2,1)S(1)}, bf16[128,1024]{1,0:T(8,128)(2,1)}, u32[]{:S(2)}) copy-start(bf16[128,1024]{1,0:T(8,128)(2,1)} %grad_ref.1) | copy-start | bytes 786436
  84.2 2.0 %copy-start.2 = (f32[128,256]{1,0:T(8,128)S(1)}, f32[128,256]{1,0:T(8,128)}, u32[]{:S(2)}) copy-start(f32[128,256]{1,0:T(8,128)} %get-tuple-element.8) | copy-start | bytes 393220
  84.2 2.6 %copy-start.1 = (f32[128,1024]{1,0:T(8,128)S(1)}, f32[128,1024]{1,0:T(8,128)}, u32[]{:S(2)}) copy-start(f32[128,1024]{1,0:T(8,128)} %get-tuple-element.13) | copy-start | bytes 1572868
